TPU v7x, 32 devices: a whole 2x2x4 slice. The times are simulated.
32 devices in a mesh: member: 2 (over y), lat: 8 (over z, x), lev: 2 (over core).
Axes of the slice: x: 2, y: 2, z: 4, core: 2. Of those that a mesh axis runs over, the one named last changes fastest.
Arguments:
- grid: bfloat16 [4, 96, 768, 1536], P('member', 'lev', 'lat'), parts along dimension 0, may hold values from -6 to 6
- w_in: bfloat16 [384, 192], replicated, may hold values from -0.4375 to 0.4375
- b_in: float32 [384], replicated, may hold values from -3 to 3
- w_out: bfloat16 [192, 384], replicated, may hold values from -0.3125 to 0.3125
- lat_weight: float32 [768], P('lat'), may hold values from 0.5 to 2
- legendre: bfloat16 [256, 513, 768], P(('lat', 'lev')), may hold values from -0.21875 to 0.21875
- order_table: int32 [256], replicated, may hold values from 0 to 255, each once
- modes: float32 [96, 96], replicated, may hold values from -0.625 to 0.625
- depths: float32 [96], replicated, may hold values from 0.05 to 2
Outputs:
- new_grid: bfloat16 [4, 96, 768, 1536], P('member', 'lev', 'lat'), parts along dimension 0
There are 2 independent parts, one for each index of `member`. A program takes and returns all parts, laid end to end along the dimension named above; an argument that names none is the same for every part. Nothing has to cross between parts.
Inputs may be any that keep to these rules, and one draw needn't show every extreme that they name: `order_table`: each of 0 to 255 appears once.
All inputs are finite; a program needn't handle non-finite values.
Results may differ from a plain program's by a relative error of at most 0.0075.
Values may be sent and summed in bfloat16 or wider, within the bound.
No kernel may reach another device: no remote copies, remote signals or barrier semaphores. Data moves between devices by JAX's collectives and lax.ppermute only.
A program may use at most 320 MiB of HBM per device.

v0:
```python
import math

import jax
import jax.numpy as jnp
from jax import lax
from jax.sharding import PartitionSpec as P

ORDERS = 512


time_step = 1.0


def fourier_table(slot_orders, lon_count, order_count):
    upper = order_count - 1 - slot_orders
    orders = jnp.stack([slot_orders, slot_orders, upper, upper], axis=-1).reshape(-1)
    parity = jnp.tile(jnp.arange(2, dtype=jnp.int32), 2 * slot_orders.shape[0])
    longitude = jnp.arange(lon_count, dtype=jnp.int32)
    phases = longitude[:, None] * orders[None, :] % lon_count
    angles = phases.astype(jnp.float32) * (2.0 * math.pi / lon_count)
    return jnp.where(parity[None, :] == 0, jnp.cos(angles), -jnp.sin(angles)).astype(jnp.bfloat16)


def implicit_update(spectral, coeff, modes, depths):
    highest = lax.Precision.HIGHEST
    modal = jnp.einsum("...l,lj->...j", spectral, modes, precision=highest)
    diverge = modal[..., 0, :, :]
    height = modal[..., 1, :, :]
    factor = coeff[..., None, None]
    updated = (diverge + time_step * factor * height) / (
        1.0 + time_step * time_step * factor * depths
    )
    raised = height - time_step * depths * updated
    both = jnp.stack([updated, raised], axis=-3)
    return jnp.einsum("...j,lj->...l", both, modes, precision=highest)


def body(grid, w_in, b_in, w_out, lat_weight, legendre, order_table, modes, depths):
    fields, half_levels, lat_rows, lon_count = grid.shape
    lat_groups = lax.axis_size("lat")
    lev_groups = lax.axis_size("lev")
    slots_dev = legendre.shape[0]
    degree_count = legendre.shape[1]
    lat_count = legendre.shape[2]
    levels = half_levels * lev_groups
    width = 4 * slots_dev
    position = lax.axis_index("lat") * lev_groups + lax.axis_index("lev")
    my_orders = lax.dynamic_slice_in_dim(order_table, position * slots_dev, slots_dev)
    weight_rows = (lat_weight * math.sqrt(2.0 / lon_count))[None, None, :, None]
    table = fourier_table(order_table, lon_count, ORDERS)
    block = lax.all_to_all(grid, "lev", split_axis=3, concat_axis=1, tiled=True)
    count_f, count_l, items, span = block.shape
    flat = block.reshape(count_f * count_l, items * span)
    hidden = jnp.dot(w_in, flat, preferred_element_type=jnp.float32) + b_in[:, None]
    hidden = jax.nn.silu(hidden).astype(jnp.bfloat16)
    change = jnp.dot(w_out, hidden, preferred_element_type=jnp.float32)
    state = lax.all_to_all(
        (flat.astype(jnp.float32) + change)
        .astype(jnp.bfloat16)
        .reshape(count_f, count_l, items, span),
        "lev",
        split_axis=1,
        concat_axis=3,
        tiled=True,
    )
    fourier = jnp.einsum("flxn,nc->flxc", state, table, preferred_element_type=jnp.float32)
    weighted = (fourier * weight_rows).astype(jnp.bfloat16)
    moved = lax.all_to_all(weighted, ("lat", "lev"), split_axis=3, concat_axis=2, tiled=True)
    moved = moved.reshape(fields, half_levels, lat_groups, lev_groups, lat_rows, width)
    moved = moved.transpose(0, 3, 1, 2, 4, 5).reshape(fields, levels, lat_count, width)
    blocks = moved.reshape(fields, levels, lat_count, slots_dev, 4)
    analysed = jnp.einsum("skx,flxsc->skfcl", legendre, blocks, preferred_element_type=jnp.float32)
    degree_index = jnp.arange(degree_count, dtype=jnp.int32)[None, :]
    first = degree_index < ORDERS - my_orders[:, None]
    first_wide = first[:, :, None, None, None]
    spectral = jnp.where(first_wide, analysed[:, :, :, 0:2], analysed[:, :, :, 2:4])
    degree = jnp.where(first, my_orders[:, None] + degree_index, degree_index - 1).astype(
        jnp.float32
    )
    coeff = degree * (degree + 1.0) / (ORDERS * ORDERS)
    updated = implicit_update(spectral, coeff, modes, depths).astype(jnp.bfloat16)
    nothing = jnp.zeros_like(updated)
    split_parts = jnp.concatenate(
        [jnp.where(first_wide, updated, nothing), jnp.where(first_wide, nothing, updated)], axis=3
    )
    band = jnp.einsum("skx,skfcl->flxsc", legendre, split_parts, preferred_element_type=jnp.float32)
    band = band.astype(jnp.bfloat16).reshape(fields, levels, lat_count, width)
    arranged = band.reshape(fields, lev_groups, half_levels, lat_groups, lat_rows, width)
    arranged = arranged.transpose(0, 2, 3, 1, 4, 5).reshape(
        fields, half_levels, lat_groups * lev_groups * lat_rows, width
    )
    returned = lax.all_to_all(arranged, ("lat", "lev"), split_axis=2, concat_axis=3, tiled=True)
    inverse_table = fourier_table(order_table, lon_count, ORDERS)
    result = jnp.einsum(
        "flxc,nc->flxn", returned, inverse_table, preferred_element_type=jnp.float32
    )
    return (result * (1.0 / math.sqrt(ORDERS))).astype(jnp.bfloat16)


def solution(mesh):
    in_specs = (
        P("member", "lev", "lat", None),
        P(),
        P(),
        P(),
        P("lat"),
        P(("lat", "lev"), None, None),
        P(),
        P(),
        P(),
    )
    out_specs = P("member", "lev", "lat", None)
    return jax.shard_map(body, mesh=mesh, in_specs=in_specs, out_specs=out_specs, check_vma=False)
```

profile of v0, /device:TPU:11, one launch (start us, length us, event | category | flops | bytes accessed | tf_op | source)
XLA Modules:
  0.0 1973.1 jit_solution(187265433367701517)
XLA Ops:
  0.0 0.0 copy-start
  0.0 43.8 %copy.28 = bf16[2,48,96,1536]{2,1,0,3:T(8,128)(2,1)} copy(bf16[2,48,96,1536]{3,2,1,0:T(8,128)(2,1)} %param.9) | data formatting | bytes 56623104 | tf_op args[0]
  43.8 64.6 %all_to_all.66 = bf16[2,48,96,1536]{2,1,0,3:T(8,128)(2,1)} all-to-all(bf16[2,48,96,1536]{2,1,0,3:T(8,128)(2,1)} %copy.28), channel_id=1, replica_groups=mesh['member'=2,'lat'=8,'lev'=2] {'lev'}, dimensions={3} | all-to-all | bytes 56623104 | tf_op jit(solution)/shard_map/all_to_all | solution.py:51
  108.4 45.0 %copy.29 = bf16[2,48,96,2,768]{4,2,1,3,0:T(8,128)(2,1)} copy(bf16[2,48,96,2,768]{2,1,0,4,3:T(8,128)(2,1)} %bitcast.87) | data formatting | bytes 56623104 | tf_op jit(solution)/shard_map/all_to_all | solution.py:51
  153.4 0.0 copy-start.9
  153.4 0.0 copy-start.10
  153.4 39.7 %copy.62 = bf16[24,8,96,768]{3,1,2,0:T(8,128)(2,1)} copy(bf16[24,8,96,768]{3,2,1,0:T(8,128)(2,1)} %bitcast.92) | data formatting | bytes 56623104
  193.1 0.0 copy-done
  193.1 0.0 copy-done.9
  193.1 0.0 copy-done.10
  193.1 56.5 %fusion.1 = bf16[192,73728]{1,0:T(8,128)(2,1)} fusion(bf16[192,384]{1,0:T(8,128)(2,1)S(1)} %copy-done, bf16[192,73728]{1,0:T(8,128)(2,1)} %bitcast.95, bf16[384,192]{0,1:T(8,128)(2,1)S(1)} %copy-done.9, f32[384]{0:T(512)S(1)} %copy-done.10), kind=kOutput, calls=%fused_computation.3 | convolution fusion | flops 21955608576 | bytes 56919552 | tf_op jit(solution)/shard_map/dot_general | solution.py:56
  249.7 19.9 %copy.63 = bf16[24,8,96,768]{3,2,1,0:T(8,128)(2,1)} copy(bf16[24,8,96,768]{3,1,2,0:T(8,128)(2,1)} %bitcast.96) | data formatting | bytes 56623104
  269.5 19.5 copy.30
  289.0 12.8 all-to-all-start.1
  301.8 21.3 %all-to-all-done.1 = bf16[2,96,96,768]{3,2,0,1:T(8,128)(2,1)} async-done(((bf16[2,96,96,768]{3,2,0,1:T(8,128)(2,1)}), bf16[2,96,96,768]{3,2,0,1:T(8,128)(2,1)}, u32[]{:S(2)}, u32[]{:S(2)}) %all-to-all-start.1) | async-done | bytes 28311584 | tf_op jit(solution)/shard_map/all_to_all | solution.py:57
  323.2 52.1 %copy.74 = bf16[2,2,48,96,768]{4,1,3,2,0:T(2,128)(2,1)} copy(bf16[2,2,48,96,768]{4,3,0,2,1:T(8,128)(2,1)} %bitcast.3) | data formatting | bytes 56623104 | tf_op jit(solution)/shard_map/all_to_all | solution.py:57
  375.2 0.0 copy-start.11
  375.2 0.0 copy-start.3
  375.2 59.8 %all_to_all.54 = bf16[2,48,96,1536]{3,2,1,0:T(8,128)(2,1)} reshape(bf16[2,48,96,2,768]{4,3,2,1,0:T(2,128)(2,1)} %bitcast.91) | data formatting | bytes 56623104 | tf_op jit(solution)/shard_map/all_to_all | solution.py:57
  435.0 0.0 copy-done.11
  435.0 0.0 copy-done.3
  435.1 0.1 copy.32
  435.2 0.1 mul.102
  435.3 0.0 copy-start.4
  435.3 0.2 eq.16
  435.5 0.0 copy-start.7
  435.5 26.5 %fusion.71 = bf16[1536,1024,1,1]{1,0,3,2:T(8,128)(2,1)S(1)} fusion(s32[1024]{0:T(1024)S(1)} %mul.102, pred[1024]{0:T(1024)(128)(4,1)S(1)} %eq.16), kind=kLoop, calls=%fused_computation.41.clone.1.clone.1 | loop fusion | flops 18874368 | bytes 3150848 | tf_op jit(solution)/shard_map/flxn,nc->flxc/dot_general | solution.py:66
  462.1 35.5 %multiply_convert_fusion.2 = bf16[2,48,96,1024]{3,2,1,0:T(8,128)(2,1)} fusion(bf16[2,48,96,1536]{3,2,1,0:T(8,128)(2,1)} %all_to_all.54, f32[96]{0:T(128)S(1)} %broadcast_multiply_fusion, bf16[1536,1024,1,1]{1,0,3,2:T(8,128)(2,1)S(1)} %fusion.71), kind=kOutput, calls=%fused_computation.5 | convolution fusion | flops 29009903616 | bytes 50332032 | tf_op jit(solution)/shard_map/flxn,nc->flxc/dot_general | solution.py:66
  497.6 0.0 copy-done.4
  497.6 0.0 copy-done.7
  497.6 29.6 %copy.33 = bf16[2,48,96,1024]{2,1,0,3:T(8,128)(2,1)} copy(bf16[2,48,96,1024]{3,2,1,0:T(8,128)(2,1)} %multiply_convert_fusion.2) | data formatting | bytes 37748736 | tf_op jit(solution)/shard_map/convert_element_type | solution.py:67
  527.2 0.0 copy-start.6
  527.2 6.7 all-to-all-start.2
  534.0 0.1 broadcast_subtract_fusion.1
  534.0 0.1 iota_compare_fusion.1
  534.1 0.1 fusion.42
  534.2 0.0 copy-done.6
  534.2 2.4 multiply_add_fusion
  536.6 539.0 %all-to-all-done.2 = bf16[2,48,96,1024]{2,1,0,3:T(8,128)(2,1)} async-done(((bf16[2,48,96,1024]{2,1,0,3:T(8,128)(2,1)}), bf16[2,48,96,1024]{2,1,0,3:T(8,128)(2,1)}, u32[]{:S(2)}, u32[]{:S(2)}) %all-to-all-start.2) | async-done | bytes 18874400 | tf_op jit(solution)/shard_map/all_to_all | solution.py:68
  1075.7 43.3 %copy.75 = bf16[2,48,8,2,96,64]{4,2,1,3,5,0:T(8,128)(2,1)} copy(bf16[2,48,8,2,96,64]{4,1,0,5,3,2:T(8,128)(2,1)} %bitcast.12) | data formatting | bytes 37748736 | tf_op jit(solution)/shard_map/reshape | solution.py:69
  1119.0 39.0 %reshape_reshape.6 = bf16[2,96,768,16,4]{2,1,4,3,0:T(8,128)(2,1)} reshape(bf16[2,2,48,8,96,64]{4,3,2,1,5,0:T(8,128)(2,1)} %bitcast.93) | data formatting | bytes 37748736 | tf_op jit(solution)/shard_map/reshape;reshape | solution.py:71
  1158.0 0.0 copy-start.2
  1158.0 32.3 %fusion.16 = f32[16,513,2,4,96]{1,4,3,2,0:T(8,128)} fusion(bf16[2,96,768,16,4]{2,1,4,3,0:T(8,128)(2,1)} %reshape_reshape.6, bf16[16,513,768,1,1]{2,0,1,4,3:T(8,128)(2,1)} %bitcast.100), kind=kOutput, calls=%fused_computation.22 | convolution fusion | flops 9682550784 | bytes 56696832 | tf_op jit(solution)/shard_map/skx,flxsc->skfcl/dot_general | solution.py:72
  1190.3 0.0 copy-done.2
  1190.3 24.3 %fusion.4 = f32[16,513,2,2,96]{1,4,3,2,0:T(8,128)} fusion(f32[16,513,2,4,96]{1,4,3,2,0:T(8,128)} %fusion.16, pred[16,513]{1,0:T(8,128)(4,1)S(1)} %iota_compare_fusion.1, f32[96,96]{1,0:T(8,128)S(1)} %copy-done.2), kind=kOutput, calls=%fused_computation.12 | convolution fusion | flops 3634108416 | bytes 37867536 | tf_op jit(solution)/shard_map/...l,lj->...j/dot_general | solution.py:26
  1214.6 11.1 multiply_subtract_fusion
  1225.7 22.3 %broadcast_select_fusion.1 = (bf16[16,513,2,2,96]{1,4,3,2,0:T(8,128)(2,1)}, bf16[16,513,2,2,96]{1,4,3,2,0:T(8,128)(2,1)}) fusion(pred[16,513]{1,0:T(8,128)(4,1)S(1)} %iota_compare_fusion.1, f32[96,96]{1,0:T(8,128)S(1)} %copy-done.2, f32[16,513,1,2,96]{1,4,3,2,0:T(8,128)S(1)} %get-tuple-element.5, f32[16,513,1,2,96]{1,4,3,2,0:T(8,128)} %get-tuple-element.6), kind=kOutput, calls=%fused_computation.30 | convolution fusion | flops 3643564032 | bytes 25260048 | tf_op jit(solution)/shard_map/...j,lj->...l/dot_general | solution.py:35
  1248.0 42.6 %convert_bitcast_fusion = bf16[2,96,768,16,4]{2,1,4,0,3:T(8,128)(2,1)} fusion(bf16[16,513,2,2,96]{1,4,3,2,0:T(8,128)(2,1)} %get-tuple-element.10, bf16[16,513,2,2,96]{1,4,3,2,0:T(8,128)(2,1)} %get-tuple-element.9, bf16[16,513,768,1,1]{2,0,1,4,3:T(8,128)(2,1)} %bitcast.101), kind=kOutput, calls=%fused_computation.10 | convolution fusion | flops 9698291712 | bytes 44089344 | tf_op jit(solution)/shard_map/skx,skfcl->flxsc/dot_general | solution.py:86
  1290.6 17.3 copy.40
  1307.9 41.9 %reshape_reshape.7 = bf16[2,2,48,8,96,64]{4,3,2,1,5,0:T(8,128)(2,1)} reshape(bf16[2,96,768,16,4]{2,1,4,3,0:T(8,128)(2,1)} %copy.40) | data formatting | bytes 37748736 | tf_op jit(solution)/shard_map/reshape;reshape | solution.py:88
  1349.8 44.9 %copy.58 = bf16[2,48,8,2,96,64]{5,1,0,4,3,2:T(8,128)(2,1)} copy(bf16[2,48,8,2,96,64]{4,2,1,3,5,0:T(8,128)(2,1)} %bitcast.94) | data formatting | bytes 37748736 | tf_op jit(solution)/shard_map/reshape | solution.py:89
  1394.7 34.4 %reshape.103 = bf16[16,2,294912]{2,1,0:T(2,128)(2,1)} reshape(bf16[1536,2,48,64]{3,2,1,0:T(8,128)(2,1)} %bitcast.88) | data formatting | bytes 37748736
  1429.1 0.0 copy-start.5
  1429.1 0.0 copy-start.8
  1429.1 5.3 all-to-all-start.3
  1434.4 0.0 copy-done.5
  1434.4 0.0 copy-done.8
  1434.4 26.5 %fusion.69 = bf16[1536,1024,1,1]{1,0,3,2:T(8,128)(2,1)S(1)} fusion(s32[1024]{0:T(1024)S(1)} %copy-done.5, pred[1024]{0:T(1024)(128)(4,1)S(1)} %copy-done.8), kind=kLoop, calls=%fused_computation.41.clone.clone.1 | loop fusion | flops 18874368 | bytes 3150848 | tf_op jit(solution)/shard_map/flxc,nc->flxn/dot_general | solution.py:94
  1460.9 380.3 %all-to-all-done.3 = bf16[16,2,294912]{2,1,0:T(2,128)(2,1)} async-done(((bf16[16,2,294912]{2,1,0:T(2,128)(2,1)}), bf16[16,2,294912]{2,1,0:T(2,128)(2,1)}, u32[]{:S(2)}, u32[]{:S(2)}) %all-to-all-start.3) | async-done | bytes 18874400 | tf_op jit(solution)/shard_map/all_to_all | solution.py:92
  1841.2 33.8 %reshape.104 = bf16[1536,2,48,64]{3,2,1,0:T(8,128)(2,1)} reshape(bf16[16,2,294912]{2,1,0:T(2,128)(2,1)} %all-to-all-done.3) | data formatting | bytes 37748736
  1875.0 46.3 %copy.44 = bf16[2,48,96,16,64]{2,4,3,1,0:T(8,128)(2,1)} copy(bf16[2,48,96,16,64]{4,1,0,2,3:T(8,128)(2,1)} %bitcast.89) | data formatting | bytes 37748736 | tf_op jit(solution)/shard_map/all_to_all | solution.py:92
  1921.2 0.0 copy-start.1
  1921.2 51.4 %multiply_convert_fusion.1 = bf16[2,48,96,1536]{3,2,1,0:T(8,128)(2,1)} fusion(bf16[2,48,96,1024]{2,3,1,0:T(8,128)(2,1)} %bitcast.97, bf16[1536,1024,1,1]{1,0,3,2:T(8,128)(2,1)S(1)} %fusion.69), kind=kOutput, calls=%fused_computation.4 | convolution fusion | flops 29019340800 | bytes 50331648 | tf_op jit(solution)/shard_map/flxc,nc->flxn/dot_general | solution.py:94
  1972.6 0.0 copy-done.1
  (5 shorter events, 0.0 us)
Async XLA Ops:
  0.0 193.1 %copy-start = (bf16[192,384]{1,0:T(8,128)(2,1)S(1)}, bf16[192,384]{1,0:T(8,128)(2,1)}, u32[]{:S(2)}) copy-start(bf16[192,384]{1,0:T(8,128)(2,1)} %param.12) | copy-start | bytes 442372
  153.4 39.7 %copy-start.9 = (bf16[384,192]{0,1:T(8,128)(2,1)S(1)}, bf16[384,192]{0,1:T(8,128)(2,1)}, u32[]{:S(2)}) copy-start(bf16[384,192]{0,1:T(8,128)(2,1)} %param.10) | copy-start | bytes 442372
  153.4 39.7 %copy-start.10 = (f32[384]{0:T(512)S(1)}, f32[384]{0:T(512)}, u32[]{:S(2)}) copy-start(f32[384]{0:T(512)} %param.11) | copy-start | bytes 4612
  289.0 34.2 %all-to-all-start.1 = ((bf16[2,96,96,768]{3,2,0,1:T(8,128)(2,1)}), bf16[2,96,96,768]{3,2,0,1:T(8,128)(2,1)}, u32[]{:S(2)}, u32[]{:S(2)}) async-start(bf16[2,96,96,768]{3,2,0,1:T(8,128)(2,1)} %copy.30), calls=%async_computation.1 | async-start | bytes 56623104 | tf_op jit(solution)/shard_map/all_to_all | solution.py:57
  375.2 59.8 %copy-start.11 = (f32[96]{0:T(128)S(1)}, f32[96]{0:T(128)}, u32[]{:S(2)}) copy-start(f32[96]{0:T(128)} %param.13) | copy-start | bytes 1156
  375.2 59.8 %copy-start.3 = (s32[256]{0:T(256)S(1)}, s32[256]{0:T(256)}, u32[]{:S(2)}) copy-start(s32[256]{0:T(256)} %param.15) | copy-start | bytes 3076
  435.3 62.3 %copy-start.4 = (s32[1024]{0:T(1024)}, s32[1024]{0:T(1024)S(1)}, u32[]{:S(2)}) copy-start(s32[1024]{0:T(1024)S(1)} %mul.102) | copy-start | bytes 12292
  435.5 62.1 %copy-start.7 = (pred[1024]{0:T(1024)(128)(4,1)}, pred[1024]{0:T(1024)(128)(4,1)S(1)}, u32[]{:S(2)}) copy-start(pred[1024]{0:T(1024)(128)(4,1)S(1)} %eq.16) | copy-start | bytes 3076
  527.2 7.0 copy-start.6
  527.2 548.5 %all-to-all-start.2 = ((bf16[2,48,96,1024]{2,1,0,3:T(8,128)(2,1)}), bf16[2,48,96,1024]{2,1,0,3:T(8,128)(2,1)}, u32[]{:S(2)}, u32[]{:S(2)}) async-start(bf16[2,48,96,1024]{2,1,0,3:T(8,128)(2,1)} %copy.33), calls=%async_computation.2 | async-start | bytes 50331648 | tf_op jit(solution)/shard_map/all_to_all | solution.py:68
  1158.0 32.3 %copy-start.2 = (f32[96,96]{1,0:T(8,128)S(1)}, f32[96,96]{1,0:T(8,128)}, u32[]{:S(2)}) copy-start(f32[96,96]{1,0:T(8,128)} %param.16) | copy-start | bytes 110596
  1429.1 5.3 copy-start.5
  1429.1 5.3 copy-start.8
  1429.1 412.1 %all-to-all-start.3 = ((bf16[16,2,294912]{2,1,0:T(2,128)(2,1)}), bf16[16,2,294912]{2,1,0:T(2,128)(2,1)}, u32[]{:S(2)}, u32[]{:S(2)}) async-start(bf16[16,2,294912]{2,1,0:T(2,128)(2,1)} %reshape.103), calls=%async_computation.3 | async-start | bytes 37748736 | tf_op jit(solution)/shard_map/all_to_all | solution.py:92
  1921.2 51.4 %copy-start.1 = (bf16[192,384]{1,0:T(8,128)(2,1)S(1)}, bf16[192,384]{1,0:T(8,128)(2,1)}, u32[]{:S(2)}) copy-start(bf16[192,384]{1,0:T(8,128)(2,1)} %param.12) | copy-start | bytes 442372
where the time goes:
time: 1990 us; the launch traced here: 1970 us
  waiting for transfers between devices  941 us (47%)
  local copies, waits for them, and re-layouts  611 us (31%)
  matrix products  265 us (13%)
  other arithmetic  66.8 us (3%)
  blocking collectives  64.6 us (3%)
  starting transfers between devices  24.8 us (1%)
    all_to_all x1, waiting for transfers between devices, body(): lax.all_to_all(weighted, ('lat', 'lev'), split_axis=3, concat_axis=2, til...  539 us
    all_to_all x1, waiting for transfers between devices, body(): lax.all_to_all(arranged, ('lat', 'lev'), split_axis=2, concat_axis=3, til...  380 us
    unnamed x29, local copies, waits for them, and re-layouts  172 us
    all_to_all x2, local copies, waits for them, and re-layouts, body(): lax.all_to_all((flat.astype(jnp.float32) + change).astype(jnp.bfloat16).r...  112 us
    all_to_all x1, blocking collectives, body(): block = lax.all_to_all(grid, 'lev', split_axis=3, concat_axis=1, tiled=True)  64.6 us
    dot_general x1, matrix products, body(): change = jnp.dot(w_out, hidden, preferred_element_type=jnp.float32)  56.5 us
    dot_general x1, matrix products, body(): jnp.einsum('flxc,nc->flxn', returned, inverse_table, preferred_element_ty...  51.4 us
    all_to_all x1, local copies, waits for them, and re-layouts, body(): lax.all_to_all(arranged, ('lat', 'lev'), split_axis=2, concat_axis=3, til...  46.3 us
  transfers between devices with their start and end apart: 3, of which 3 were waited for; matrix products, arithmetic and copies ran while one was open for 1% of the time, Pallas kernels for 0%

commit v1 on v0

--- a/solution.py
+++ b/solution.py
@@ -1,11 +1,19 @@
+import functools
 import math
 
 import jax
 import jax.numpy as jnp
+import numpy as np
 from jax import lax
+from jax.experimental import pallas as pl
+from jax.experimental.pallas import tpu as pltpu
 from jax.sharding import PartitionSpec as P
 
 ORDERS = 512
+ROWS = 16
+LANES = 128
+BF16 = jnp.bfloat16
+F32 = jnp.float32
 
 
 time_step = 1.0
@@ -35,7 +43,7 @@
     return jnp.einsum("...j,lj->...l", both, modes, precision=highest)
 
 
-def body(grid, w_in, b_in, w_out, lat_weight, legendre, order_table, modes, depths):
+def plain_body(grid, w_in, b_in, w_out, lat_weight, legendre, order_table, modes, depths):
     fields, half_levels, lat_rows, lon_count = grid.shape
     lat_groups = lax.axis_size("lat")
     lev_groups = lax.axis_size("lev")
@@ -97,6 +105,416 @@
     return (result * (1.0 / math.sqrt(ORDERS))).astype(jnp.bfloat16)
 
 
+def analysis_lanes(fields, half_levels):
+    count = 2 * fields * half_levels
+    tail = count - LANES
+    part = np.concatenate([np.repeat([0, 1], LANES), np.repeat([0, 1], tail)])
+    item = np.concatenate([np.tile(np.arange(LANES), 2), np.tile(LANES + np.arange(tail), 2)])
+    half, rest = np.divmod(item, fields * half_levels)
+    field, level = np.divmod(rest, half_levels)
+    return part, field, half * half_levels + level
+
+
+def synthesis_lanes(fields, half_levels):
+    half, order, part, field, level = np.meshgrid(
+        np.arange(2), np.arange(2), np.arange(2), np.arange(fields), np.arange(half_levels), indexing="ij"
+    )
+    return part.reshape(-1), field.reshape(-1), (half * half_levels + level).reshape(-1)
+
+
+def split_wide(x):
+    high = x.astype(BF16)
+    return high, (x - high.astype(F32)).astype(BF16)
+
+
+def mode_matrices(modes, fields, half_levels):
+    levels = modes.shape[0]
+    padded = jnp.pad(modes, ((0, 0), (0, LANES - levels)))
+    modal_field = np.repeat(np.arange(fields), 2 * LANES)
+    modal_part = np.tile(np.repeat([0, 1], LANES), fields)
+
+    def matrix(lanes):
+        part, field, level = lanes
+        keep = (part[:, None] == modal_part[None, :]) & (field[:, None] == modal_field[None, :])
+        rows = jnp.take(padded, jnp.asarray(level), axis=0)
+        return jnp.where(jnp.asarray(keep), jnp.tile(rows, (1, 2 * fields)), 0.0)
+
+    to_modal = matrix(analysis_lanes(fields, half_levels))
+    to_levels = matrix(synthesis_lanes(fields, half_levels)).T
+    return split_wide(to_modal), split_wide(to_levels)
+
+
+def table_kernel(ca_ref, sa_ref, cb_ref, sb_ref, out_ref):
+    half = ca_ref.shape[0] // 2
+    for block in range(ca_ref.shape[1]):
+        lanes = slice(block * LANES, (block + 1) * LANES)
+        ca, sa = ca_ref[:, block : block + 1], sa_ref[:, block : block + 1]
+        cb, sb = cb_ref[...], sb_ref[...]
+        cos = (ca * cb - sa * sb).astype(BF16)
+        sin = -(sa * cb + ca * sb).astype(BF16)
+        out_ref[0, :, lanes] = cos[:half]
+        out_ref[1, :, lanes] = sin[:half]
+        out_ref[2, :, lanes] = cos[half:]
+        out_ref[3, :, lanes] = sin[half:]
+
+
+def transposed_table(order_table, lon_count):
+    orders = jnp.concatenate([order_table, ORDERS - 1 - order_table]).astype(jnp.int32)
+    coarse = jnp.arange(lon_count // LANES, dtype=jnp.int32) * LANES
+    fine = jnp.arange(LANES, dtype=jnp.int32)
+    scale = 2.0 * math.pi / lon_count
+    angle_a = (orders[:, None] * coarse[None, :] % lon_count).astype(F32) * scale
+    angle_b = (orders[:, None] * fine[None, :] % lon_count).astype(F32) * scale
+    return pl.pallas_call(
+        table_kernel,
+        out_shape=jax.ShapeDtypeStruct((4, order_table.shape[0], lon_count), BF16),
+        compiler_params=pltpu.CompilerParams(vmem_limit_bytes=40 << 20),
+        name="table",
+    )(jnp.cos(angle_a), jnp.sin(angle_a), jnp.cos(angle_b), jnp.sin(angle_b))
+
+
+def forward_kernel(
+    split, core_ref, weight_ref, own_ref, other_ref, w_in_ref, b_in_ref, w_out_ref, table_ref, *refs
+):
+    outs, state, packed = refs[:-2], refs[-2], refs[-1]
+    step = pl.program_id(0)
+    core = core_ref[0]
+    half = own_ref.shape[0]
+    lon_count = own_ref.shape[2]
+    slots = table_ref.shape[1]
+    own_at = pl.multiple_of(core * half, 32)
+    other_at = pl.multiple_of((1 - core) * half, 32)
+    state[:, pl.ds(own_at, half), :] = jnp.swapaxes(own_ref[...], 0, 1)
+    state[:, pl.ds(other_at, half), :] = jnp.swapaxes(other_ref[...], 0, 1)
+    span = 512
+    lane = lax.broadcasted_iota(jnp.int32, (slots, LANES), 1)
+
+    def row(r, carry):
+        for start in range(0, lon_count, span):
+            lons = slice(start, start + span)
+            values = state[r, : 2 * half, lons]
+            hidden = jnp.dot(w_in_ref[...], values, preferred_element_type=F32) + b_in_ref[...]
+            hidden = (hidden * (0.5 + 0.5 * jnp.tanh(0.5 * hidden))).astype(BF16)
+            change = jnp.dot(w_out_ref[...], hidden, preferred_element_type=F32)
+            doubled = jnp.concatenate([values, values[LANES:]], axis=0).astype(F32)
+            state[r, :, lons] = (doubled + change).astype(BF16)
+        weight = weight_ref[step * ROWS + r]
+        for order in range(2):
+            parts = []
+            for part in range(2):
+                fourier = lax.dot_general(
+                    table_ref[2 * order + part],
+                    state[r],
+                    (((1,), (1,)), ((), ())),
+                    preferred_element_type=F32,
+                )
+                parts.append(fourier * weight)
+            real, imag = parts
+            base = order * 3 * LANES
+            packed[r, :, base : base + LANES] = real[:, :LANES].astype(BF16)
+            packed[r, :, base + LANES : base + 2 * LANES] = imag[:, :LANES].astype(BF16)
+            mixed = jnp.where(lane < LANES // 2, real[:, LANES:], imag[:, LANES:])
+            packed[r, :, base + 2 * LANES : base + 3 * LANES] = mixed.astype(BF16)
+        return carry
+
+    lax.fori_loop(0, ROWS, row, 0)
+    if not split:
+        outs[0][...] = jnp.swapaxes(packed[...], 0, 1)
+    else:
+        own_slots = split
+        part_slots = own_slots // 2
+        for position in range(slots // own_slots):
+            for index in range(2):
+                start = position * own_slots + index * part_slots
+                block = packed[:, start : start + part_slots, :]
+                outs[index][position * part_slots : (position + 1) * part_slots] = jnp.swapaxes(
+                    block, 0, 1
+                )
+
+
+def forward(split, core, weights, grid, first_block, other, w_in, b_in, w_out, table):
+    half, rows, lon_count = other.shape
+    slots = table.shape[1]
+    hidden = w_in.shape[0]
+    lanes = 6 * LANES
+    if split:
+        outs = [jax.ShapeDtypeStruct((slots // 2, rows, lanes), BF16)] * 2
+    else:
+        outs = [jax.ShapeDtypeStruct((slots, rows, lanes), BF16)]
+    once = pl.Buffered(1)
+    whole = lambda shape: pl.BlockSpec(shape, lambda i, *_: (0,) * len(shape), pipeline_mode=once)
+    flops = 2 * rows * lon_count * (2 * 2 * half * hidden + 2 * half * 4 * slots)
+    return pl.pallas_call(
+        functools.partial(forward_kernel, split),
+        grid_spec=pltpu.PrefetchScalarGridSpec(
+            num_scalar_prefetch=2,
+            grid=(rows // ROWS,),
+            in_specs=[
+                pl.BlockSpec(
+                    (half, ROWS, lon_count),
+                    lambda i, core, weights: (0, first_block(core[0]) + i, 0),
+                    pipeline_mode=once,
+                ),
+                pl.BlockSpec((half, ROWS, lon_count), lambda i, *_: (0, i, 0), pipeline_mode=once),
+                whole(w_in.shape),
+                whole(b_in.shape),
+                whole(w_out.shape),
+                whole(table.shape),
+            ],
+            out_specs=[pl.BlockSpec((o.shape[0], ROWS, lanes), lambda i, *_: (0, i, 0)) for o in outs],
+            scratch_shapes=[
+                pltpu.VMEM((ROWS, 2 * LANES, lon_count), BF16),
+                pltpu.VMEM((ROWS, slots, lanes), BF16),
+            ],
+        ),
+        out_shape=outs,
+        compiler_params=pltpu.CompilerParams(vmem_limit_bytes=58 << 20),
+        cost_estimate=pl.CostEstimate(
+            flops=3 * flops, bytes_accessed=rows * (4 * half * lon_count + 2 * slots * lanes), transcendentals=0
+        ),
+        name="forward",
+    )(core, weights, grid, other, w_in, b_in, w_out, table)
+
+
+def spectral_kernel(
+    last_rows, order_ref, first_ref, second_ref, legendre_ref, to_modal_h, to_modal_l, to_levels_h, to_levels_l,
+    depth_ref, main_ref, last_ref, blocks,
+):
+    order = order_ref[pl.program_id(0)]
+    sources, _, first_rows, lanes = first_ref.shape
+    second_rows = second_ref.shape[2]
+    own_rows = first_rows + second_rows
+    for source in range(sources):
+        at = source * own_rows
+        blocks[at : at + first_rows] = first_ref[source, 0]
+        blocks[at + first_rows : at + own_rows] = second_ref[source, 0]
+    legendre = legendre_ref[0]
+    degrees = legendre.shape[0]
+    analysed = jnp.dot(legendre, blocks[...], preferred_element_type=F32)
+    index = lax.broadcasted_iota(jnp.int32, (degrees, 1), 0)
+    first = index < ORDERS - order
+    spectral = jnp.where(first, analysed[:, : lanes // 2], analysed[:, lanes // 2 :])
+    degree = jnp.where(first, order + index, index - 1).astype(F32)
+    coeff = degree * (degree + 1.0) / (ORDERS * ORDERS)
+
+    def product(values, high, low):
+        top, rest = split_wide(values)
+        return (
+            jnp.dot(top, high[...], preferred_element_type=F32)
+            + jnp.dot(rest, high[...], preferred_element_type=F32)
+            + jnp.dot(top, low[...], preferred_element_type=F32)
+        )
+
+    modal = product(spectral, to_modal_h, to_modal_l)
+    width = modal.shape[1] // 2
+    diverge, height = modal[:, :width], modal[:, width:]
+    depth = depth_ref[...]
+    updated = (diverge + time_step * coeff * height) / (1.0 + time_step * time_step * coeff * depth)
+    raised = height - time_step * depth * updated
+    both = jnp.concatenate([updated, raised], axis=1)
+    values = product(both, to_levels_h, to_levels_l)
+    lane = lax.broadcasted_iota(jnp.int32, (1, lanes), 1)
+    group = lanes // 4
+    of_first = (lane < group) | ((lane >= 2 * group) & (lane < 3 * group))
+    values = jnp.where(first == of_first, values, 0.0).astype(BF16)
+    band = lax.dot_general(
+        legendre, values, (((0,), (0,)), ((), ())), preferred_element_type=F32
+    ).astype(BF16)
+    lat_rows = 2 * own_rows
+    main_rows = lat_rows - last_rows
+    for place in range(sources // 2):
+        for half in range(2):
+            piece = band[place * lat_rows : (place + 1) * lat_rows, half * (lanes // 2) : (half + 1) * (lanes // 2)]
+            main_ref[2 * place + half, 0] = piece[:main_rows]
+            last_ref[2 * place + half, 0] = piece[main_rows:]
+
+
+def spectral_step(part, last_rows, orders, first, second, legendre, to_modal, to_levels, depths):
+    sources, slots, second_rows, lanes = second.shape
+    first_rows = first.shape[2]
+    _, degrees, lat_count = legendre.shape
+    lat_rows = 2 * (first_rows + second_rows)
+    main_rows = lat_rows - last_rows
+    once = pl.Buffered(1)
+    whole = lambda shape: pl.BlockSpec(shape, lambda s, *_: (0,) * len(shape), pipeline_mode=once)
+    modal = to_modal[0].shape[1]
+    macs = slots * degrees * (2 * lat_count * lanes + 3 * modal * (lanes // 2 + lanes))
+    return pl.pallas_call(
+        functools.partial(spectral_kernel, last_rows),
+        grid_spec=pltpu.PrefetchScalarGridSpec(
+            num_scalar_prefetch=1,
+            grid=(slots,),
+            in_specs=[
+                pl.BlockSpec((sources, 1, first_rows, lanes), lambda s, _: (0, part * slots + s, 0, 0)),
+                pl.BlockSpec((sources, 1, second_rows, lanes), lambda s, _: (0, s, 0, 0)),
+                pl.BlockSpec((1, degrees, lat_count), lambda s, _: (part * slots + s, 0, 0)),
+                whole(to_modal[0].shape),
+                whole(to_modal[1].shape),
+                whole(to_levels[0].shape),
+                whole(to_levels[1].shape),
+                whole(depths.shape),
+            ],
+            out_specs=[
+                pl.BlockSpec((sources, 1, main_rows, lanes // 2), lambda s, _: (0, s, 0, 0)),
+                pl.BlockSpec((sources, 1, last_rows, lanes // 2), lambda s, _: (0, s, 0, 0)),
+            ],
+            scratch_shapes=[pltpu.VMEM((lat_count, lanes), BF16)],
+        ),
+        out_shape=[
+            jax.ShapeDtypeStruct((sources, slots, main_rows, lanes // 2), BF16),
+            jax.ShapeDtypeStruct((sources, slots, last_rows, lanes // 2), BF16),
+        ],
+        compiler_params=pltpu.CompilerParams(vmem_limit_bytes=50 << 20),
+        cost_estimate=pl.CostEstimate(
+            flops=4 * macs, bytes_accessed=2 * slots * lat_count * (2 * lanes + degrees), transcendentals=0
+        ),
+        name="spectral",
+    )(orders, first, second, legendre, *to_modal, *to_levels, depths)
+
+
+def inverse_kernel(scale, *refs):
+    bands, table_ref, out_ref, columns = refs[:-4], refs[-4], refs[-2], refs[-1]
+    items = out_ref.shape[0]
+    at = 0
+    total = sum(b.shape[0] for b in bands)
+    for band in bands:
+        slots = band.shape[0]
+        rows = jnp.swapaxes(band[...], 0, 1)
+        for r in range(ROWS):
+            turned = rows[r].T
+            for q in range(4):
+                columns[r, :, q * total + at : q * total + at + slots] = turned[q * items : (q + 1) * items]
+        at += slots
+    left = jnp.swapaxes(columns[...], 0, 1).reshape(items * ROWS, columns.shape[2])
+    result = jnp.dot(left, table_ref[...], preferred_element_type=F32) * scale
+    out_ref[...] = result.astype(BF16).reshape(out_ref.shape)
+
+
+def inverse_kernel_first(scale, *refs):
+    inverse_kernel(scale, *refs[:-2], None, *refs[-2:])
+
+
+def inverse(bands, table, lat_rows, first_row, target):
+    rows, lanes = bands[0].shape[1:]
+    items = lanes // 4
+    lon_count = table.shape[1]
+    columns = table.shape[0]
+    scale = 1.0 / math.sqrt(ORDERS)
+    first_block = first_row // ROWS
+    operands = list(bands) + [table]
+    in_specs = [pl.BlockSpec((b.shape[0], ROWS, lanes), lambda i: (0, i, 0)) for b in bands]
+    in_specs.append(pl.BlockSpec(table.shape, lambda i: (0, 0), pipeline_mode=pl.Buffered(1)))
+    aliases = {}
+    kernel = inverse_kernel_first
+    if target is not None:
+        aliases = {len(operands): 0}
+        operands.append(target)
+        in_specs.append(pl.BlockSpec(memory_space=pl.ANY))
+        kernel = inverse_kernel
+    return pl.pallas_call(
+        functools.partial(kernel, scale),
+        grid=(rows // ROWS,),
+        in_specs=in_specs,
+        out_specs=pl.BlockSpec((items, ROWS, lon_count), lambda i: (0, first_block + i, 0)),
+        out_shape=jax.ShapeDtypeStruct((items, lat_rows, lon_count), BF16),
+        scratch_shapes=[pltpu.VMEM((ROWS, items, columns), BF16)],
+        input_output_aliases=aliases,
+        compiler_params=pltpu.CompilerParams(vmem_limit_bytes=58 << 20),
+        cost_estimate=pl.CostEstimate(
+            flops=4 * rows * items * columns * lon_count,
+            bytes_accessed=2 * rows * (columns * items + items * lon_count),
+            transcendentals=0,
+        ),
+        name="inverse",
+    )(*operands)
+
+
+def tiled_body(grid, w_in, b_in, w_out, lat_weight, legendre, order_table, modes, depths):
+    fields, half_levels, lat_rows, lon_count = grid.shape
+    slots_dev, degree_count, lat_count = legendre.shape
+    levels = 2 * half_levels
+    half = fields * half_levels
+    own_rows = lat_rows // 2
+    core = lax.axis_index("lev")
+    position = lax.axis_index("lat") * 2 + core
+    positions = lax.axis_size("lat") * 2
+    everyone = ("lat", "lev")
+    flat = grid.reshape(half, lat_rows, lon_count)
+    core_word = core.astype(jnp.int32).reshape(1)
+    swap = [(0, 1), (1, 0)]
+
+    def swapped(start, rows):
+        piece = lax.dynamic_slice_in_dim(flat, (1 - core) * own_rows + start, rows, 1)
+        return lax.ppermute(piece, "lev", swap)
+
+    first_rows = ROWS
+    second_rows = own_rows - first_rows
+    other_first = swapped(0, first_rows)
+    other_second = swapped(first_rows, second_rows)
+
+    hidden = w_in.shape[0]
+    w_in_own = w_in.reshape(hidden, fields, 2, half_levels).transpose(0, 2, 1, 3).reshape(hidden, 2 * half)
+    w_out_own = w_out.reshape(fields, 2, half_levels, hidden).transpose(1, 0, 2, 3).reshape(2 * half, hidden)
+    w_out_own = jnp.concatenate([w_out_own, w_out_own[LANES:]], axis=0)
+    weights = lax.dynamic_slice_in_dim(lat_weight * math.sqrt(2.0 / lon_count), core * own_rows, own_rows)
+    table = transposed_table(order_table, lon_count)
+    network = (w_in_own, b_in[:, None], w_out_own, table)
+    own_blocks = own_rows // ROWS
+
+    (all_slots,) = forward(
+        0, core_word, weights[:first_rows], flat, lambda c: c * own_blocks, other_first, *network
+    )
+    parts = forward(
+        slots_dev, core_word, weights[first_rows:], flat, lambda c: c * own_blocks + 1, other_second, *network
+    )
+
+    def send(x):
+        shape = (positions, x.size // (positions * x.shape[-2] * x.shape[-1])) + x.shape[-2:]
+        return lax.all_to_all(x.reshape(shape), everyone, split_axis=0, concat_axis=0, tiled=True)
+
+    got_first = send(all_slots)
+    my_orders = lax.dynamic_slice_in_dim(order_table, position * slots_dev, slots_dev)
+    part_slots = slots_dev // 2
+    to_modal, to_levels = mode_matrices(modes, fields, half_levels)
+    depth_lanes = jnp.tile(jnp.pad(depths, (0, LANES - levels)), 2)[None, :]
+    last_rows = ROWS
+    mains, lasts = [], []
+    for part in range(2):
+        got = send(parts[part])
+        orders = my_orders[part * part_slots : (part + 1) * part_slots]
+        main, last = spectral_step(
+            part, last_rows, orders, got_first, got, legendre, to_modal, to_levels, depth_lanes
+        )
+        mains.append(send(main))
+        lasts.append(last)
+    last = send(jnp.concatenate(lasts, axis=1))
+    split_table = table.reshape(4, positions, 2, part_slots, lon_count)
+    halves = split_table.transpose(0, 2, 1, 3, 4).reshape(4 * positions * slots_dev, lon_count)
+    plain = table.reshape(4 * positions * slots_dev, lon_count)
+    join = lambda x: x.reshape((x.shape[0] * x.shape[1],) + x.shape[2:])
+    result = inverse([join(m) for m in mains], halves, lat_rows, 0, None)
+    result = inverse([join(last)], plain, lat_rows, lat_rows - last_rows, result)
+    return result.reshape(grid.shape)
+
+
+def body(grid, w_in, b_in, w_out, lat_weight, legendre, order_table, modes, depths):
+    fields, half_levels, lat_rows, lon_count = grid.shape
+    slots_dev = legendre.shape[0]
+    count = 2 * fields * half_levels
+    tiled = (
+        lax.axis_size("lev") == 2
+        and lat_rows % (2 * ROWS) == 0
+        and lat_rows >= 4 * ROWS
+        and count == LANES + LANES // 2
+        and half_levels * 2 <= LANES
+        and half_levels % ROWS == 0
+        and lon_count % 512 == 0
+        and slots_dev % 16 == 0
+    )
+    chosen = tiled_body if tiled else plain_body
+    return chosen(grid, w_in, b_in, w_out, lat_weight, legendre, order_table, modes, depths)
+
+
 def solution(mesh):
     in_specs = (
         P("member", "lev", "lat", None),

time: 1990 us -> 948 us (0.48)
  local copies, waits for them, and re-layouts: 611 us -> 40.9 us
  waiting for transfers between devices: 941 us -> 419 us
  Pallas kernels: 0 us -> 302 us
  matrix products: 265 us -> 0 us
  blocking collectives: 64.6 us -> 142 us
  other arithmetic: 66.8 us -> 5.65 us
    all_to_all x3 -> x5, waiting for transfers between devices: 941 us -> 419 us  [send(): lax.all_to_all(x.reshape(shape), everyone, split_axis=0, concat_axis=0, t...]
    pallas_call x0 -> x7, Pallas kernels: none -> 302 us  [the longest x2 140 us: forward(): pl.pallas_call(functools.partial(forward_kernel, split), grid_spec=pltpu....]
    dot_general x7 -> x0, matrix products: 265 us -> none  [the longest x1 56.5 us: body(): change = jnp.dot(w_out, hidden, preferred_element_type=jnp.float32)]
    all_to_all x4 -> x0, local copies, waits for them, and re-layouts: 203 us -> none  [the longest x2 112 us: body(): lax.all_to_all((flat.astype(jnp.float32) + change).astype(jnp.bfloat16).r...]
    unnamed x29 -> x47, local copies, waits for them, and re-layouts: 172 us -> 19.5 us
    reshape x3, local copies, waits for them, and re-layouts: 108 us -> 2.83 us  [the longest x1 1.99 us: tiled_body(): split_table = table.reshape(4, positions, 2, part_slots, lon_count)]
    another operation x3 -> x1, local copies, waits for them, and re-layouts: 81 us -> 0.01 us  [tiled_body(): depth_lanes = jnp.tile(jnp.pad(depths, (0, LANES - levels)), 2)[None, :]]
    all_to_all x1, blocking collectives: 64.6 us -> 142 us  [send(): lax.all_to_all(x.reshape(shape), everyone, split_axis=0, concat_axis=0, t...]
  transfers between devices with their start and end apart: 3 -> 7, of which waited for: 3 -> 5; matrix products, arithmetic and copies ran while one was open for 1% -> 4% of each run, Pallas kernels for 0% -> 31%
where the time goes in v1:
time: 948 us; the launch traced here: 939 us
  waiting for transfers between devices  419 us (44%)
  Pallas kernels  302 us (32%)
  blocking collectives  142 us (15%)
  local copies, waits for them, and re-layouts  40.9 us (4%)
  starting transfers between devices  28.6 us (3%)
    all_to_all x5, waiting for transfers between devices, send(): lax.all_to_all(x.reshape(shape), everyone, split_axis=0, concat_axis=0, t...  419 us
    all_to_all x1, blocking collectives, send(): lax.all_to_all(x.reshape(shape), everyone, split_axis=0, concat_axis=0, t...  142 us
    pallas_call x2, Pallas kernels, forward(): pl.pallas_call(functools.partial(forward_kernel, split), grid_spec=pltpu....  140 us
    pallas_call x2, Pallas kernels, spectral_step(): pl.pallas_call(functools.partial(spectral_kernel, last_rows), grid_spec=p...  113 us
    pallas_call x2, Pallas kernels, inverse(): pl.pallas_call(functools.partial(kernel, scale), grid=(rows // ROWS,), in...  47.5 us
    all_to_all x5, starting transfers between devices, send(): lax.all_to_all(x.reshape(shape), everyone, split_axis=0, concat_axis=0, t...  27.9 us
    unnamed x47, local copies, waits for them, and re-layouts  19.5 us
  transfers between devices with their start and end apart: 7, of which 5 were waited for; matrix products, arithmetic and copies ran while one was open for 4% of the time, Pallas kernels for 31%

profile of v1, /device:TPU:11, one launch (start us, length us, event | category | flops | bytes accessed | tf_op | source)
XLA Modules:
  0.0 939.0 jit_solution(17686901146909225561)
XLA Ops:
  0.0 0.0 copy-start
  0.0 4.9 constant_dynamic-slice_fusion.1
  4.9 0.7 collective-permute-start
  5.6 0.0 copy-start.19
  5.6 8.7 constant_dynamic-slice_fusion
  14.3 0.0 collective-permute-start.1
  14.3 0.0 copy-done.12
  14.3 0.8 copy.43.w_in_ref
  15.2 0.0 copy-done.13
  15.2 0.0 copy-done.17
  15.2 0.8 broadcast_in_dim.48.b_in_ref
  16.0 0.0 copy-done.15
  16.0 0.1 fusion.9
  16.1 0.1 copy.42
  16.3 0.0 copy-done.19
  16.3 0.6 dynamic_slice.13
  16.9 1.1 fusion.6
  18.0 1.0 multiply_sine_fusion
  19.0 1.8 table.1.table_ref
  20.8 0.0 copy-start.2
  20.8 1.6 copy-done.2
  22.4 0.7 pad_maximum_fusion.1.w_out_ref
  23.1 0.0 collective-permute-done.other_ref
  23.1 47.3 %forward.2 = bf16[256,16,768]{2,1,0:T(8,128)(2,1)} custom-call(s32[1]{0:T(128)} %bitcast.core_ref, f32[16]{0:T(128)} %bitcast.62, bf16[96,96,1536]{2,1,0:T(8,128)(2,1)} %bitcast.51, bf16[96,16,1536]{2,1,0:T(8,128)(2,1)} %collective-permute-done.other_ref, bf16[384,192]{1,0:T(8,128)(2,1)} %copy.43.w_in_ref, f32[384,1]{1,0:T(8,128)} %broadcast_in_dim.48.b_in_ref, ...), custom_call_target="tpu_custom_call" | custom-call | flops 50734301184 | bytes 15728640 | tf_op jit(solution)/shard_map/forward/pallas_call | solution.py:247
  70.4 6.8 all-to-all-start
  77.2 0.6 slice.18.weight_ref
  77.8 0.0 collective-permute-done.1.other_ref
  77.8 92.6 %forward.3 = (bf16[128,32,768]{2,1,0:T(8,128)(2,1)}, bf16[128,32,768]{2,1,0:T(8,128)(2,1)}) custom-call(s32[1]{0:T(128)} %bitcast.core_ref, f32[32]{0:T(128)} %slice.18.weight_ref, bf16[96,96,1536]{2,1,0:T(8,128)(2,1)} %bitcast.52, bf16[96,32,1536]{2,1,0:T(8,128)(2,1)} %collective-permute-done.1.other_ref, bf16[384,192]{1,0:T(8,128)(2,1)} %copy.43.w_in_ref, ...), custom_call_target="tpu_custom_call" | custom-call | flops 101468602368 | bytes 31457280 | tf_op jit(solution)/shard_map/forward/pallas_call | solution.py:247
  170.4 44.1 %all-to-all-done.first_ref = bf16[16,16,16,768]{3,2,1,0:T(8,128)(2,1)} async-done(((bf16[16,16,16,768]{3,2,1,0:T(8,128)(2,1)}), bf16[16,16,16,768]{3,2,1,0:T(8,128)(2,1)}, u32[]{:S(2)}, u32[]{:S(2)}) %all-to-all-start) | async-done | bytes 6291488 | tf_op jit(solution)/shard_map/all_to_all | solution.py:473
  214.5 142.2 %all_to_all.30.second_ref = bf16[16,8,32,768]{3,2,1,0:T(8,128)(2,1)} all-to-all(bf16[16,8,32,768]{3,2,1,0:T(8,128)(2,1)} %bitcast.55), channel_id=1, replica_groups=mesh['member'=2,'lat'=8,'lev'=2] {'lat','lev'}, dimensions={0} | all-to-all | bytes 12582912 | tf_op jit(solution)/shard_map/all_to_all | solution.py:473
  356.6 6.0 all-to-all-start.1
  362.7 0.0 copy-start.11
  362.7 0.1 dynamic_slice.12
  362.8 0.0 copy-done.20
  362.8 1.1 gather_fusion
  364.0 1.6 gather_fusion.1
  365.6 0.2 copy.51
  365.8 0.3 broadcast_select_fusion.1
  366.1 0.1 copy.57
  366.2 0.0 copy-start.10
  366.2 12.1 %copy.48.legendre_ref = bf16[16,513,768]{2,1,0:T(8,128)(2,1)} copy(bf16[16,513,768]{2,0,1:T(8,128)(2,1)} %param.18) | data formatting | bytes 25214976 | tf_op args[5]
  378.3 0.1 fusion.13
  378.3 0.1 fusion.1.to_modal_l
  378.4 0.2 broadcast_select_fusion
  378.6 0.1 fusion
  378.7 0.5 copy-done.8
  379.2 56.4 %spectral.3 = (bf16[16,8,80,384]{3,2,1,0:T(8,128)(2,1)}, bf16[16,8,16,384]{3,2,1,0:T(8,128)(2,1)S(1)}) custom-call(s32[8]{0:T(128)S(1)} %get-tuple-element.24.order_ref, bf16[16,16,16,768]{3,2,1,0:T(8,128)(2,1)} %all-to-all-done.first_ref, bf16[16,8,32,768]{3,2,1,0:T(8,128)(2,1)} %all_to_all.30.second_ref, bf16[16,513,768]{2,1,0:T(8,128)(2,1)} %copy.48.legendre_ref, ...), custom_call_target="tpu_custom_call" | custom-call | flops 48412753920 | bytes 25178112 | tf_op jit(solution)/shard_map/spectral/pallas_call | solution.py:342
  435.6 0.9 copy-done.4
  436.5 0.9 copy-done.6
  437.4 62.5 %all-to-all-done.1.second_ref = bf16[16,8,32,768]{3,2,1,0:T(8,128)(2,1)} async-done(((bf16[16,8,32,768]{3,2,1,0:T(8,128)(2,1)}), bf16[16,8,32,768]{3,2,1,0:T(8,128)(2,1)}, u32[]{:S(2)}, u32[]{:S(2)}) %all-to-all-start.1) | async-done | bytes 6291488 | tf_op jit(solution)/shard_map/all_to_all | solution.py:473
  499.9 4.9 all-to-all-start.5
  504.8 1.1 copy-done.5
  505.9 1.1 copy-done.7
  507.1 1.0 copy-done.9
  508.1 56.2 %spectral.2 = (bf16[16,8,80,384]{3,2,1,0:T(8,128)(2,1)}, bf16[16,8,16,384]{3,2,1,0:T(8,128)(2,1)S(1)}) custom-call(s32[8]{0:T(128)S(1)} %get-tuple-element.23.order_ref, bf16[16,16,16,768]{3,2,1,0:T(8,128)(2,1)} %all-to-all-done.first_ref, bf16[16,8,32,768]{3,2,1,0:T(8,128)(2,1)} %all-to-all-done.1.second_ref, bf16[16,513,768]{2,1,0:T(8,128)(2,1)} %copy.48.legendre_ref, ...), custom_call_target="tpu_custom_call" | custom-call | flops 48412753920 | bytes 25178112 | tf_op jit(solution)/shard_map/spectral/pallas_call | solution.py:342
  564.3 111.6 %all-to-all-done.5 = bf16[16,8,80,384]{3,2,1,0:T(8,128)(2,1)} async-done(((bf16[16,8,80,384]{3,2,1,0:T(8,128)(2,1)}), bf16[16,8,80,384]{3,2,1,0:T(8,128)(2,1)}, u32[]{:S(2)}, u32[]{:S(2)}) %all-to-all-start.5) | async-done | bytes 7864352 | tf_op jit(solution)/shard_map/all_to_all | solution.py:473
  675.9 5.3 all-to-all-start.4
  681.2 2.1 pad_maximum_fusion
  683.3 168.9 %all-to-all-done.4 = bf16[16,8,80,384]{3,2,1,0:T(8,128)(2,1)} async-done(((bf16[16,8,80,384]{3,2,1,0:T(8,128)(2,1)}), bf16[16,8,80,384]{3,2,1,0:T(8,128)(2,1)}, u32[]{:S(2)}, u32[]{:S(2)}) %all-to-all-start.4) | async-done | bytes 7864352 | tf_op jit(solution)/shard_map/all_to_all | solution.py:473
  852.2 4.9 all-to-all-start.3
  857.1 2.0 copy.50
  859.1 36.1 %inverse.2.refs_2_ = bf16[96,96,1536]{2,1,0:T(8,128)(2,1)} custom-call(bf16[128,80,384]{2,1,0:T(8,128)(2,1)} %bitcast.18.refs_0_, bf16[128,80,384]{2,1,0:T(8,128)(2,1)} %bitcast.19.refs_1_, bf16[1024,1536]{1,0:T(8,128)(2,1)} %bitcast.56), custom_call_target="tpu_custom_call" | custom-call | flops 48318382080 | bytes 39321600 | tf_op jit(solution)/shard_map/inverse/pallas_call | solution.py:414
  895.1 31.9 %all-to-all-done.3 = bf16[16,16,16,384]{3,2,1,0:T(8,128)(2,1)} async-done(((bf16[16,16,16,384]{3,2,1,0:T(8,128)(2,1)}), bf16[16,16,16,384]{3,2,1,0:T(8,128)(2,1)}, u32[]{:S(2)}, u32[]{:S(2)}) %all-to-all-start.3) | async-done | bytes 3145760 | tf_op jit(solution)/shard_map/all_to_all | solution.py:473
  927.1 11.4 %inverse.3 = bf16[96,96,1536]{2,1,0:T(8,128)(2,1)} custom-call(bf16[256,16,384]{2,1,0:T(8,128)(2,1)} %bitcast.16.refs_0_, bf16[1024,1536]{1,0:T(8,128)(2,1)} %bitcast.41, bf16[96,96,1536]{2,1,0:T(8,128)(2,1)} %inverse.2.refs_2_), custom_call_target="tpu_custom_call", output_to_operand_aliasing={{}: (2, {})} | custom-call | flops 9663676416 | bytes 7864320 | tf_op jit(solution)/shard_map/inverse/pallas_call | solution.py:414
  (39 shorter events, 0.2 us)
Async XLA Ops:
  0.0 362.8 %copy-start = (f32[96,96]{1,0:T(8,128)S(1)}, f32[96,96]{1,0:T(8,128)}, u32[]{:S(2)}) copy-start(f32[96,96]{1,0:T(8,128)} %param.20) | copy-start | bytes 110596
  4.9 18.2 %collective-permute-start = (bf16[96,16,1536]{2,1,0:T(8,128)(2,1)}, bf16[96,16,1536]{2,1,0:T(8,128)(2,1)}, u32[]{:S(2)}, u32[]{:S(2)}) collective-permute-start(bf16[96,16,1536]{2,1,0:T(8,128)(2,1)} %constant_dynamic-slice_fusion.1), channel_id=1, source_target_pairs={{0,1},{1,0},{2,3},{3,2},{4,5},{5,4},{6,7},{7,6},{8,9},{9,8},{10,11... | collective-permute-start | bytes 14155784 | tf_op jit(solution)/shard_map/ppermute | solution.py:448
  5.6 8.7 copy-start.12
  5.6 9.6 %copy-start.13 = (bf16[192,384]{1,0:T(8,128)(2,1)S(1)}, bf16[192,384]{1,0:T(8,128)(2,1)}, u32[]{:S(2)}) copy-start(bf16[192,384]{1,0:T(8,128)(2,1)} %param.16) | copy-start | bytes 442372
  5.6 9.6 %copy-start.17 = (f32[384]{0:T(512)S(1)}, f32[384]{0:T(512)}, u32[]{:S(2)}) copy-start(f32[384]{0:T(512)} %param.15) | copy-start | bytes 4612
  5.6 10.4 %copy-start.15 = (s32[256]{0:T(256)S(1)}, s32[256]{0:T(256)}, u32[]{:S(2)}) copy-start(s32[256]{0:T(256)} %param.19) | copy-start | bytes 3076
  5.6 10.7 %copy-start.19 = (f32[96]{0:T(128)S(1)}, f32[96]{0:T(128)}, u32[]{:S(2)}) copy-start(f32[96]{0:T(128)} %param.17) | copy-start | bytes 1156
  14.3 63.5 %collective-permute-start.1 = (bf16[96,32,1536]{2,1,0:T(8,128)(2,1)}, bf16[96,32,1536]{2,1,0:T(8,128)(2,1)}, u32[]{:S(2)}, u32[]{:S(2)}) collective-permute-start(bf16[96,32,1536]{2,1,0:T(8,128)(2,1)} %constant_dynamic-slice_fusion), channel_id=1, source_target_pairs={{0,1},{1,0},{2,3},{3,2},{4,5},{5,4},{6,7},{7,6},{8,9},{9,8},{10,11... | collective-permute-start | bytes 28311560 | tf_op jit(solution)/shard_map/ppermute | solution.py:448
  20.8 1.6 copy-start.2
  70.4 6.8 copy-start.21
  70.4 144.1 %all-to-all-start = ((bf16[16,16,16,768]{3,2,1,0:T(8,128)(2,1)}), bf16[16,16,16,768]{3,2,1,0:T(8,128)(2,1)}, u32[]{:S(2)}, u32[]{:S(2)}) async-start(bf16[16,16,16,768]{3,2,1,0:T(8,128)(2,1)} %bitcast.54), calls=%async_computation | async-start | bytes 12582912 | tf_op jit(solution)/shard_map/all_to_all | solution.py:473
  356.6 6.0 copy-start.16
  356.6 6.1 copy-start.20
  356.6 6.1 copy-start.18
  356.6 7.3 copy-start.14
  356.6 143.3 %all-to-all-start.1 = ((bf16[16,8,32,768]{3,2,1,0:T(8,128)(2,1)}), bf16[16,8,32,768]{3,2,1,0:T(8,128)(2,1)}, u32[]{:S(2)}, u32[]{:S(2)}) async-start(bf16[16,8,32,768]{3,2,1,0:T(8,128)(2,1)} %bitcast.53), calls=%async_computation.1 | async-start | bytes 12582912 | tf_op jit(solution)/shard_map/all_to_all | solution.py:473
  362.7 3.1 copy-start.11
  366.2 12.2 %copy-start.10 = (pred[768,4,128]{0,2,1:T(32,128)(4,1)S(1)}, pred[768,4,128]{0,2,1:T(32,128)(4,1)}, u32[]{:S(2)}) copy-start(pred[768,4,128]{0,2,1:T(32,128)(4,1)} %constant.114) | copy-start | bytes 1179652
  378.4 0.8 copy-start.8
  435.6 0.9 copy-start.4
  436.5 0.9 copy-start.6
  499.9 176.0 %all-to-all-start.5 = ((bf16[16,8,80,384]{3,2,1,0:T(8,128)(2,1)}), bf16[16,8,80,384]{3,2,1,0:T(8,128)(2,1)}, u32[]{:S(2)}, u32[]{:S(2)}) async-start(bf16[16,8,80,384]{3,2,1,0:T(8,128)(2,1)} %get-tuple-element.16), calls=%async_computation.5 | async-start | bytes 15728640 | tf_op jit(solution)/shard_map/all_to_all | solution.py:473
  504.8 1.1 copy-start.5
  505.9 1.1 copy-start.7
  507.1 1.0 copy-start.9
  675.9 176.3 %all-to-all-start.4 = ((bf16[16,8,80,384]{3,2,1,0:T(8,128)(2,1)}), bf16[16,8,80,384]{3,2,1,0:T(8,128)(2,1)}, u32[]{:S(2)}, u32[]{:S(2)}) async-start(bf16[16,8,80,384]{3,2,1,0:T(8,128)(2,1)} %get-tuple-element.15), calls=%async_computation.4 | async-start | bytes 15728640 | tf_op jit(solution)/shard_map/all_to_all | solution.py:473
  683.3 173.8 %copy-start.3 = (bf16[4,256,1536]{2,1,0:T(8,128)(2,1)S(1)}, bf16[4,256,1536]{2,1,0:T(8,128)(2,1)}, u32[]{:S(2)}) copy-start(bf16[4,256,1536]{2,1,0:T(8,128)(2,1)} %copy-done.2) | copy-start | bytes 9437188
  852.2 74.9 %all-to-all-start.3 = ((bf16[16,16,16,384]{3,2,1,0:T(8,128)(2,1)}), bf16[16,16,16,384]{3,2,1,0:T(8,128)(2,1)}, u32[]{:S(2)}, u32[]{:S(2)}) async-start(bf16[16,16,16,384]{3,2,1,0:T(8,128)(2,1)} %pad_maximum_fusion), calls=%async_computation.3 | async-start | bytes 6291456 | tf_op jit(solution)/shard_map/all_to_all | solution.py:473
  927.1 11.4 %copy-start.1 = (f32[96,96]{1,0:T(8,128)S(1)}, f32[96,96]{1,0:T(8,128)}, u32[]{:S(2)}) copy-start(f32[96,96]{1,0:T(8,128)} %param.20) | copy-start | bytes 110596

commit v2 on v1

v2 whole, which is shorter than its diff:
```python
import functools
import math

import jax
import jax.numpy as jnp
import numpy as np
from jax import lax
from jax.experimental import pallas as pl
from jax.experimental.pallas import tpu as pltpu
from jax.sharding import PartitionSpec as P

ORDERS = 512
ROWS = 16
LANES = 128
BF16 = jnp.bfloat16
F32 = jnp.float32


time_step = 1.0


def fourier_table(slot_orders, lon_count, order_count):
    upper = order_count - 1 - slot_orders
    orders = jnp.stack([slot_orders, slot_orders, upper, upper], axis=-1).reshape(-1)
    parity = jnp.tile(jnp.arange(2, dtype=jnp.int32), 2 * slot_orders.shape[0])
    longitude = jnp.arange(lon_count, dtype=jnp.int32)
    phases = longitude[:, None] * orders[None, :] % lon_count
    angles = phases.astype(jnp.float32) * (2.0 * math.pi / lon_count)
    return jnp.where(parity[None, :] == 0, jnp.cos(angles), -jnp.sin(angles)).astype(jnp.bfloat16)


def implicit_update(spectral, coeff, modes, depths):
    highest = lax.Precision.HIGHEST
    modal = jnp.einsum("...l,lj->...j", spectral, modes, precision=highest)
    diverge = modal[..., 0, :, :]
    height = modal[..., 1, :, :]
    factor = coeff[..., None, None]
    updated = (diverge + time_step * factor * height) / (
        1.0 + time_step * time_step * factor * depths
    )
    raised = height - time_step * depths * updated
    both = jnp.stack([updated, raised], axis=-3)
    return jnp.einsum("...j,lj->...l", both, modes, precision=highest)


def plain_body(grid, w_in, b_in, w_out, lat_weight, legendre, order_table, modes, depths):
    fields, half_levels, lat_rows, lon_count = grid.shape
    lat_groups = lax.axis_size("lat")
    lev_groups = lax.axis_size("lev")
    slots_dev = legendre.shape[0]
    degree_count = legendre.shape[1]
    lat_count = legendre.shape[2]
    levels = half_levels * lev_groups
    width = 4 * slots_dev
    position = lax.axis_index("lat") * lev_groups + lax.axis_index("lev")
    my_orders = lax.dynamic_slice_in_dim(order_table, position * slots_dev, slots_dev)
    weight_rows = (lat_weight * math.sqrt(2.0 / lon_count))[None, None, :, None]
    table = fourier_table(order_table, lon_count, ORDERS)
    block = lax.all_to_all(grid, "lev", split_axis=3, concat_axis=1, tiled=True)
    count_f, count_l, items, span = block.shape
    flat = block.reshape(count_f * count_l, items * span)
    hidden = jnp.dot(w_in, flat, preferred_element_type=jnp.float32) + b_in[:, None]
    hidden = jax.nn.silu(hidden).astype(jnp.bfloat16)
    change = jnp.dot(w_out, hidden, preferred_element_type=jnp.float32)
    state = lax.all_to_all(
        (flat.astype(jnp.float32) + change)
        .astype(jnp.bfloat16)
        .reshape(count_f, count_l, items, span),
        "lev",
        split_axis=1,
        concat_axis=3,
        tiled=True,
    )
    fourier = jnp.einsum("flxn,nc->flxc", state, table, preferred_element_type=jnp.float32)
    weighted = (fourier * weight_rows).astype(jnp.bfloat16)
    moved = lax.all_to_all(weighted, ("lat", "lev"), split_axis=3, concat_axis=2, tiled=True)
    moved = moved.reshape(fields, half_levels, lat_groups, lev_groups, lat_rows, width)
    moved = moved.transpose(0, 3, 1, 2, 4, 5).reshape(fields, levels, lat_count, width)
    blocks = moved.reshape(fields, levels, lat_count, slots_dev, 4)
    analysed = jnp.einsum("skx,flxsc->skfcl", legendre, blocks, preferred_element_type=jnp.float32)
    degree_index = jnp.arange(degree_count, dtype=jnp.int32)[None, :]
    first = degree_index < ORDERS - my_orders[:, None]
    first_wide = first[:, :, None, None, None]
    spectral = jnp.where(first_wide, analysed[:, :, :, 0:2], analysed[:, :, :, 2:4])
    degree = jnp.where(first, my_orders[:, None] + degree_index, degree_index - 1).astype(
        jnp.float32
    )
    coeff = degree * (degree + 1.0) / (ORDERS * ORDERS)
    updated = implicit_update(spectral, coeff, modes, depths).astype(jnp.bfloat16)
    nothing = jnp.zeros_like(updated)
    split_parts = jnp.concatenate(
        [jnp.where(first_wide, updated, nothing), jnp.where(first_wide, nothing, updated)], axis=3
    )
    band = jnp.einsum("skx,skfcl->flxsc", legendre, split_parts, preferred_element_type=jnp.float32)
    band = band.astype(jnp.bfloat16).reshape(fields, levels, lat_count, width)
    arranged = band.reshape(fields, lev_groups, half_levels, lat_groups, lat_rows, width)
    arranged = arranged.transpose(0, 2, 3, 1, 4, 5).reshape(
        fields, half_levels, lat_groups * lev_groups * lat_rows, width
    )
    returned = lax.all_to_all(arranged, ("lat", "lev"), split_axis=2, concat_axis=3, tiled=True)
    inverse_table = fourier_table(order_table, lon_count, ORDERS)
    result = jnp.einsum(
        "flxc,nc->flxn", returned, inverse_table, preferred_element_type=jnp.float32
    )
    return (result * (1.0 / math.sqrt(ORDERS))).astype(jnp.bfloat16)


def analysis_lanes(fields, half_levels):
    count = 2 * fields * half_levels
    tail = count - LANES
    part = np.concatenate([np.repeat([0, 1], LANES), np.repeat([0, 1], tail)])
    item = np.concatenate([np.tile(np.arange(LANES), 2), np.tile(LANES + np.arange(tail), 2)])
    half, rest = np.divmod(item, fields * half_levels)
    field, level = np.divmod(rest, half_levels)
    return part, field, half * half_levels + level


def synthesis_lanes(fields, half_levels):
    group = 2 * fields * half_levels
    tail = group - LANES
    half = np.concatenate([np.repeat([0, 1], LANES), np.repeat([0, 1], tail)])
    item = np.concatenate([np.tile(np.arange(LANES), 2), np.tile(LANES + np.arange(tail), 2)])
    part, rest = np.divmod(item, fields * half_levels)
    field, level = np.divmod(rest, half_levels)
    return part, field, half * half_levels + level


def split_wide(x):
    high = x.astype(BF16)
    return high, (x - high.astype(F32)).astype(BF16)


def mode_matrices(modes, fields, half_levels):
    levels = modes.shape[0]
    padded = jnp.pad(modes, ((0, 0), (0, LANES - levels)))
    modal_field = np.repeat(np.arange(fields), 2 * LANES)
    modal_part = np.tile(np.repeat([0, 1], LANES), fields)

    def matrix(lanes):
        part, field, level = lanes
        keep = (part[:, None] == modal_part[None, :]) & (field[:, None] == modal_field[None, :])
        rows = jnp.take(padded, jnp.asarray(level), axis=0)
        return jnp.where(jnp.asarray(keep), jnp.tile(rows, (1, 2 * fields)), 0.0)

    to_modal = matrix(analysis_lanes(fields, half_levels))
    to_levels = matrix(synthesis_lanes(fields, half_levels)).T
    return split_wide(to_modal), split_wide(to_levels)


def cost(flops, bytes_accessed, transcendentals):
    return pl.CostEstimate(
        flops=flops // 32, bytes_accessed=bytes_accessed // 16, transcendentals=transcendentals
    )


def table_kernel(ca_ref, sa_ref, cb_ref, sb_ref, out_ref):
    half = ca_ref.shape[0] // 2
    for block in range(ca_ref.shape[1]):
        lanes = slice(block * LANES, (block + 1) * LANES)
        ca, sa = ca_ref[:, block : block + 1], sa_ref[:, block : block + 1]
        cb, sb = cb_ref[...], sb_ref[...]
        cos = (ca * cb - sa * sb).astype(BF16)
        sin = -(sa * cb + ca * sb).astype(BF16)
        out_ref[0, :, lanes] = cos[:half]
        out_ref[1, :, lanes] = sin[:half]
        out_ref[2, :, lanes] = cos[half:]
        out_ref[3, :, lanes] = sin[half:]


def transposed_table(order_table, lon_count):
    orders = jnp.concatenate([order_table, ORDERS - 1 - order_table]).astype(jnp.int32)
    coarse = jnp.arange(lon_count // LANES, dtype=jnp.int32) * LANES
    fine = jnp.arange(LANES, dtype=jnp.int32)
    scale = 2.0 * math.pi / lon_count
    angle_a = (orders[:, None] * coarse[None, :] % lon_count).astype(F32) * scale
    angle_b = (orders[:, None] * fine[None, :] % lon_count).astype(F32) * scale
    return pl.pallas_call(
        table_kernel,
        out_shape=jax.ShapeDtypeStruct((4, order_table.shape[0], lon_count), BF16),
        compiler_params=pltpu.CompilerParams(vmem_limit_bytes=40 << 20),
        name="table",
    )(jnp.cos(angle_a), jnp.sin(angle_a), jnp.cos(angle_b), jnp.sin(angle_b))


def forward_kernel(core_ref, weight_ref, own_ref, other_ref, w_in_ref, b_in_ref, w_out_ref, table_ref, *refs):
    outs, (columns, packed, even, odd) = refs[:-4], refs[-4:]
    core = core_ref[0]
    half = own_ref.shape[0]
    lon_count = own_ref.shape[2]
    slots = table_ref.shape[1]
    own_at = pl.multiple_of(core * half, 32)
    other_at = pl.multiple_of((1 - core) * half, 32)
    columns[:, pl.ds(own_at, half), :] = jnp.swapaxes(own_ref[...], 0, 1)
    columns[:, pl.ds(other_at, half), :] = jnp.swapaxes(other_ref[...], 0, 1)
    lane = lax.broadcasted_iota(jnp.int32, (slots, LANES), 1)

    def network(r, state):
        values = columns[r]
        hidden = jnp.dot(w_in_ref[...], values, preferred_element_type=F32) + b_in_ref[...]
        hidden = (hidden + hidden * jnp.tanh(hidden)).astype(BF16)
        change = jnp.dot(w_out_ref[...], hidden, preferred_element_type=F32)
        result = (values.astype(F32) + change).astype(BF16)
        state[: 2 * half] = result
        state[2 * half :] = result[LANES:]

    def transform(r, state):
        weight = weight_ref[pl.program_id(0) * ROWS + r]
        fourier = lax.dot_general(
            table_ref[...].reshape(4 * slots, lon_count),
            state[...],
            (((1,), (1,)), ((), ())),
            preferred_element_type=F32,
        )
        for order in range(2):
            at = 2 * order * slots
            real = fourier[at : at + slots] * weight
            imag = fourier[at + slots : at + 2 * slots] * weight
            base = order * 3 * LANES
            packed[r, :, base : base + LANES] = real[:, :LANES].astype(BF16)
            packed[r, :, base + LANES : base + 2 * LANES] = imag[:, :LANES].astype(BF16)
            mixed = jnp.where(lane < LANES // 2, real[:, LANES:], imag[:, LANES:])
            packed[r, :, base + 2 * LANES : base + 3 * LANES] = mixed.astype(BF16)

    network(0, even)

    def two_rows(i, carry):
        network(2 * i + 1, odd)
        transform(2 * i, even)
        network(jnp.minimum(2 * i + 2, ROWS - 1), even)
        transform(2 * i + 1, odd)
        return carry

    lax.fori_loop(0, ROWS // 2, two_rows, 0)
    at = 0
    for out in outs:
        out[...] = jnp.swapaxes(packed[:, at : at + out.shape[0], :], 0, 1)
        at += out.shape[0]


def forward(links, link_slots, core, weights, grid, first_block, other, w_in, b_in, w_out, table):
    half, rows, lon_count = other.shape
    slots = table.shape[1]
    hidden = w_in.shape[0]
    lanes = 6 * LANES
    outs = [jax.ShapeDtypeStruct((link_slots, rows, lanes), BF16)] * links
    outs.append(jax.ShapeDtypeStruct((slots - links * link_slots, rows, lanes), BF16))
    once = pl.Buffered(1)
    whole = lambda shape: pl.BlockSpec(shape, lambda i, *_: (0,) * len(shape), pipeline_mode=once)
    flops = 2 * rows * lon_count * (2 * 2 * half * hidden + 2 * half * 4 * slots)
    return pl.pallas_call(
        forward_kernel,
        grid_spec=pltpu.PrefetchScalarGridSpec(
            num_scalar_prefetch=2,
            grid=(rows // ROWS,),
            in_specs=[
                pl.BlockSpec(
                    (half, ROWS, lon_count),
                    lambda i, core, weights: (0, first_block(core[0]) + i, 0),
                    pipeline_mode=once,
                ),
                pl.BlockSpec((half, ROWS, lon_count), lambda i, *_: (0, i, 0), pipeline_mode=once),
                whole(w_in.shape),
                whole(b_in.shape),
                whole(w_out.shape),
                whole(table.shape),
            ],
            out_specs=[pl.BlockSpec((o.shape[0], ROWS, lanes), lambda i, *_: (0, i, 0)) for o in outs],
            scratch_shapes=[
                pltpu.VMEM((ROWS, 2 * half, lon_count), BF16),
                pltpu.VMEM((ROWS, slots, lanes), BF16),
                pltpu.VMEM((2 * LANES, lon_count), BF16),
                pltpu.VMEM((2 * LANES, lon_count), BF16),
            ],
        ),
        out_shape=outs,
        compiler_params=pltpu.CompilerParams(vmem_limit_bytes=58 << 20),
        cost_estimate=cost(
            flops=3 * flops, bytes_accessed=rows * (4 * half * lon_count + 2 * slots * lanes), transcendentals=0
        ),
        name="forward",
    )(core, weights, grid, other, w_in, b_in, w_out, table)


def select_orders(order, analysed):
    lanes = analysed.shape[1] // 2
    index = lax.broadcasted_iota(jnp.int32, (analysed.shape[0], 1), 0)
    return jnp.where(index < ORDERS - order, analysed[:, :lanes], analysed[:, lanes:])


def product(values, high, low):
    top, rest = split_wide(values)
    return (
        jnp.dot(top, high[...], preferred_element_type=F32)
        + jnp.dot(rest, high[...], preferred_element_type=F32)
        + jnp.dot(top, low[...], preferred_element_type=F32)
    )


def implicit_lanes(order, spectral, to_modal_h, to_modal_l, to_levels_h, to_levels_l, depth_ref):
    index = lax.broadcasted_iota(jnp.int32, (spectral.shape[0], 1), 0)
    degree = jnp.where(index < ORDERS - order, order + index, index - 1).astype(F32)
    coeff = degree * (degree + 1.0) / (ORDERS * ORDERS)
    modal = product(spectral, to_modal_h, to_modal_l)
    width = modal.shape[1] // 2
    diverge, height = modal[:, :width], modal[:, width:]
    depth = depth_ref[...]
    updated = (diverge + time_step * coeff * height) / (1.0 + time_step * time_step * coeff * depth)
    raised = height - time_step * depth * updated
    both = jnp.concatenate([updated, raised], axis=1)
    return product(both, to_levels_h, to_levels_l).astype(BF16)


def band_halves(order, legendre, values):
    lanes = values.shape[1]
    index = lax.broadcasted_iota(jnp.int32, (values.shape[0], 1), 0)
    first = index < ORDERS - order
    nothing = jnp.zeros_like(values)
    both = jnp.concatenate([jnp.where(first, values, nothing), jnp.where(first, nothing, values)], axis=1)
    band = lax.dot_general(legendre, both, (((0,), (0,)), ((), ())), preferred_element_type=F32)
    lane = lax.broadcasted_iota(jnp.int32, (1, LANES), 1)
    low = lane < LANES // 2
    rest_a, rest_b = band[:, 2 * LANES : lanes], band[:, lanes + 2 * LANES :]
    rests = [
        jnp.where(low, rest_a, pltpu.roll(rest_b, LANES // 2, 1)),
        jnp.where(low, pltpu.roll(rest_a, LANES // 2, 1), rest_b),
    ]
    halves = []
    for half in range(2):
        a = band[:, half * LANES : (half + 1) * LANES]
        b = band[:, lanes + half * LANES : lanes + (half + 1) * LANES]
        halves.append(jnp.concatenate([a, b, rests[half]], axis=1).astype(BF16))
    return halves


def full_kernel(chunks, order_ref, *refs):
    pieces, (legendre_ref, *matrices), (main_ref, last_ref, blocks) = (
        refs[:chunks],
        refs[chunks:-3],
        refs[-3:],
    )
    order = order_ref[pl.program_id(0)]
    sources = pieces[0].shape[0]
    own_rows = blocks.shape[0] // sources
    for source in range(sources):
        at = source * own_rows
        for piece in pieces:
            blocks[at : at + piece.shape[2]] = piece[source, 0]
            at += piece.shape[2]
    legendre = legendre_ref[0]
    spectral = select_orders(order, jnp.dot(legendre, blocks[...], preferred_element_type=F32))
    halves = band_halves(order, legendre, implicit_lanes(order, spectral, *matrices))
    lat_rows = 2 * own_rows
    main_rows = main_ref.shape[2]
    for place in range(sources // 2):
        for half in range(2):
            piece = halves[half][place * lat_rows : (place + 1) * lat_rows]
            main_ref[2 * place + half, 0] = piece[:main_rows]
            last_ref[2 * place + half, 0] = piece[main_rows:]


def whole_once(shape):
    return pl.BlockSpec(shape, lambda s, *_: (0,) * len(shape), pipeline_mode=pl.Buffered(1))


def spectral_full(first_slot, last_rows, orders, pieces, legendre, matrices):
    sources, slots, _, lanes = pieces[0].shape
    _, degrees, lat_count = legendre.shape
    lat_rows = 2 * lat_count // sources
    main_rows = lat_rows - last_rows
    macs = slots * degrees * (2 * lat_count * lanes + 3 * 4 * LANES * lanes)
    shapes = [(sources, slots, rows, lanes // 2) for rows in (main_rows, last_rows)]
    return pl.pallas_call(
        functools.partial(full_kernel, len(pieces)),
        grid_spec=pltpu.PrefetchScalarGridSpec(
            num_scalar_prefetch=1,
            grid=(slots,),
            in_specs=[pl.BlockSpec((sources, 1, p.shape[2], lanes), lambda s, _: (0, s, 0, 0)) for p in pieces]
            + [pl.BlockSpec((1, degrees, lat_count), lambda s, _: (first_slot + s, 0, 0))]
            + [whole_once(m.shape) for m in matrices],
            out_specs=[
                pl.BlockSpec((sources, 1) + shape[2:], lambda s, _: (0, s, 0, 0)) for shape in shapes
            ],
            scratch_shapes=[pltpu.VMEM((lat_count, lanes), BF16)],
        ),
        out_shape=[jax.ShapeDtypeStruct(shape, BF16) for shape in shapes],
        compiler_params=pltpu.CompilerParams(vmem_limit_bytes=50 << 20),
        cost_estimate=cost(
            flops=4 * macs, bytes_accessed=2 * slots * lat_count * (2 * lanes + degrees), transcendentals=0
        ),
        name="spectral_full",
    )(orders, *pieces, legendre, *matrices)


def gather_half(place, pieces, blocks):
    masks = len(pieces[0])
    own_rows = blocks.shape[0] // masks
    for mask in range(masks):
        done = 0
        for chunk_pieces in pieces:
            rows = chunk_pieces[mask].shape[1]
            at = pl.multiple_of((place ^ mask) * own_rows + done, ROWS)
            blocks[pl.ds(at, rows)] = chunk_pieces[mask][0]
            done += rows


def partial_kernel(chunks, first_slot, place_ref, order_ref, *refs):
    masks = (len(refs) - 3) // chunks
    pieces = [refs[c * masks : (c + 1) * masks] for c in range(chunks)]
    legendre_ref, out_ref, blocks = refs[-3:]
    gather_half(place_ref[0], pieces, blocks)
    order = order_ref[first_slot + pl.program_id(0)]
    analysed = jnp.dot(legendre_ref[0], blocks[...], preferred_element_type=F32)
    out_ref[0] = select_orders(order, analysed).astype(BF16)


def update_kernel(chunks, first_slot, place_ref, order_ref, *refs):
    masks = (len(refs) - 9) // chunks
    pieces = [refs[c * masks : (c + 1) * masks] for c in range(chunks)]
    legendre_ref, got_ref, *matrices, out_ref, blocks = refs[chunks * masks :]
    gather_half(place_ref[0], pieces, blocks)
    order = order_ref[first_slot + pl.program_id(0)]
    analysed = jnp.dot(legendre_ref[0], blocks[...], preferred_element_type=F32)
    spectral = select_orders(order, analysed) + got_ref[0].astype(F32)
    out_ref[0] = implicit_lanes(order, spectral, *matrices)


def spectral_half(first_slot, slots, place, orders, pieces, legendre, got, matrices):
    flat = [array for chunk in pieces for array, _ in chunk]
    bases = [base for chunk in pieces for _, base in chunk]
    lanes = flat[0].shape[2]
    _, degrees, lat_count = legendre.shape
    at_slot = lambda shape, base=0: pl.BlockSpec(
        (1,) + shape, lambda s, *_: (base + first_slot + s, 0, 0)
    )
    plain = pl.BlockSpec((1, degrees, lanes // 2), lambda s, *_: (s, 0, 0))
    macs = slots * degrees * lat_count * lanes
    operands = flat + [legendre]
    in_specs = [at_slot(x.shape[1:], base) for x, base in zip(flat, bases)] + [at_slot((degrees, lat_count))]
    kernel = partial_kernel
    if got is not None:
        kernel = update_kernel
        operands += [got, *matrices]
        in_specs += [plain] + [whole_once(m.shape) for m in matrices]
        macs += slots * degrees * 3 * 4 * LANES * lanes
    return pl.pallas_call(
        functools.partial(kernel, len(pieces), first_slot),
        grid_spec=pltpu.PrefetchScalarGridSpec(
            num_scalar_prefetch=2,
            grid=(slots,),
            in_specs=in_specs,
            out_specs=plain,
            scratch_shapes=[pltpu.VMEM((lat_count, lanes), BF16)],
        ),
        out_shape=jax.ShapeDtypeStruct((slots, degrees, lanes // 2), BF16),
        compiler_params=pltpu.CompilerParams(vmem_limit_bytes=50 << 20),
        cost_estimate=cost(
            flops=4 * macs, bytes_accessed=2 * slots * lat_count * (lanes + degrees), transcendentals=0
        ),
        name="spectral_partial" if got is None else "spectral_update",
    )(place, orders, *operands)


def synthesis_kernel(first_slot, place_ref, order_ref, legendre_ref, values_ref, *refs):
    outs, bands = refs[:-1], refs[-1]
    order = order_ref[first_slot + pl.program_id(0)]
    halves = band_halves(order, legendre_ref[0], values_ref[0])
    lat_rows = bands.shape[1]
    for place in range(len(outs)):
        for half in range(2):
            bands[2 * place + half] = halves[half][place * lat_rows : (place + 1) * lat_rows]
    for link, out in enumerate(outs):
        for other in range(2):
            out[other, 0] = bands[place_ref[0] ^ (2 * link + other)]


def synthesis_half(first_slot, masks, place, orders, legendre, values):
    slots, degrees, lanes = values.shape
    lat_count = legendre.shape[2]
    lat_rows = 2 * lat_count // masks
    return pl.pallas_call(
        functools.partial(synthesis_kernel, first_slot),
        grid_spec=pltpu.PrefetchScalarGridSpec(
            num_scalar_prefetch=2,
            grid=(slots,),
            in_specs=[
                pl.BlockSpec((1, degrees, lat_count), lambda s, *_: (first_slot + s, 0, 0)),
                pl.BlockSpec((1, degrees, lanes), lambda s, *_: (s, 0, 0)),
            ],
            out_specs=[pl.BlockSpec((2, 1, lat_rows, lanes), lambda s, *_: (0, s, 0, 0))] * (masks // 2),
            scratch_shapes=[pltpu.VMEM((masks, lat_rows, lanes), BF16)],
        ),
        out_shape=[jax.ShapeDtypeStruct((2, slots, lat_rows, lanes), BF16)] * (masks // 2),
        compiler_params=pltpu.CompilerParams(vmem_limit_bytes=50 << 20),
        cost_estimate=cost(
            flops=8 * slots * degrees * lat_count * lanes,
            bytes_accessed=2 * slots * lat_count * (lanes + degrees),
            transcendentals=0,
        ),
        name="synthesis_half",
    )(place, orders, legendre, values)


def inverse_kernel(scale, *refs):
    bands, table_ref, out_ref, columns = refs[:-4], refs[-4], refs[-2], refs[-1]
    items = out_ref.shape[0]
    together = jnp.concatenate([band[...] for band in bands], axis=0)
    total = together.shape[0]
    rows = jnp.swapaxes(together, 0, 1)
    cut = 2 * LANES
    for r in range(ROWS):
        turned = rows[r].T
        for order in range(2):
            begin, rest = order * LANES, cut + order * (LANES // 2)
            both = jnp.concatenate([turned[begin : begin + LANES], turned[rest : rest + LANES // 2]], axis=0)
            for part in range(2):
                at = (2 * order + part) * total
                columns[r, :, at : at + total] = both[part * items : (part + 1) * items]
    left = jnp.swapaxes(columns[...], 0, 1).reshape(items * ROWS, columns.shape[2])
    result = jnp.dot(left, table_ref[...], preferred_element_type=F32) * scale
    out_ref[...] = result.astype(BF16).reshape(out_ref.shape)


def inverse_kernel_first(scale, *refs):
    inverse_kernel(scale, *refs[:-2], None, *refs[-2:])


def inverse(bands, rows, table, lat_rows, first_row, target):
    lanes = bands[0][0].shape[2]
    items = lanes // 4
    columns, lon_count = table.shape
    scale = 1.0 / math.sqrt(ORDERS)
    first_block = first_row // ROWS
    operands = [band[0] for band in bands] + [table]
    in_specs = [
        pl.BlockSpec((slots, ROWS, lanes), lambda i, block=block, at=start // ROWS: (block, at + i, 0))
        for _, slots, block, start in bands
    ]
    in_specs.append(pl.BlockSpec(table.shape, lambda i: (0, 0), pipeline_mode=pl.Buffered(1)))
    aliases = {}
    kernel = inverse_kernel_first
    if target is not None:
        aliases = {len(operands): 0}
        operands.append(target)
        in_specs.append(pl.BlockSpec(memory_space=pl.ANY))
        kernel = inverse_kernel
    return pl.pallas_call(
        functools.partial(kernel, scale),
        grid=(rows // ROWS,),
        in_specs=in_specs,
        out_specs=pl.BlockSpec((items, ROWS, lon_count), lambda i: (0, first_block + i, 0)),
        out_shape=jax.ShapeDtypeStruct((items, lat_rows, lon_count), BF16),
        scratch_shapes=[pltpu.VMEM((ROWS, items, columns), BF16)],
        input_output_aliases=aliases,
        compiler_params=pltpu.CompilerParams(vmem_limit_bytes=58 << 20),
        cost_estimate=cost(
            flops=4 * rows * items * columns * lon_count,
            bytes_accessed=2 * rows * (columns * items + items * lon_count),
            transcendentals=0,
        ),
        name="inverse",
    )(*operands)


def tiled_body(grid, w_in, b_in, w_out, lat_weight, legendre, order_table, modes, depths):
    fields, half_levels, lat_rows, lon_count = grid.shape
    slots_dev, degree_count, lat_count = legendre.shape
    levels = 2 * half_levels
    half = fields * half_levels
    own_rows = lat_rows // 2
    own_blocks = own_rows // ROWS
    chunks = [(at * ROWS, ROWS) for at in range(own_blocks)]
    core = lax.axis_index("lev")
    position = lax.axis_index("lat") * 2 + core
    positions = lax.axis_size("lat") * 2
    masks = positions // 2
    mirror = position ^ masks
    place = (position % masks).astype(jnp.int32).reshape(1)
    side = position // masks
    everyone = ("lat", "lev")
    join = lambda x: x.reshape((x.shape[0] * x.shape[1],) + x.shape[2:])
    pairs = lambda mask: [(p, p ^ mask) for p in range(positions)]
    shift = lambda x, mask: lax.ppermute(x, everyone, pairs(mask)) if mask else x
    flat = grid.reshape(half, lat_rows, lon_count)
    core_word = core.astype(jnp.int32).reshape(1)

    def cut_rows(start, rows, core):
        return lax.dynamic_slice_in_dim(flat, (1 - core) * own_rows + start, rows, 1)

    def swapped(piece):
        return lax.ppermute(piece, "lev", [(0, 1), (1, 0)])

    batch = slots_dev // 4
    pair = 2 * batch
    links = masks // 2
    half_lats = lat_count // 2
    turn = lax.axis_index("member") % 2
    members = lax.axis_size("member")
    piece, core = lax.optimization_barrier((cut_rows(*chunks[0], core), core))
    others = [swapped(piece)]
    share = batch // 2
    crossing = lax.dynamic_slice(
        legendre, (turn * share, 0, (1 - side) * half_lats), (share, degree_count, half_lats)
    )
    core, crossing = lax.optimization_barrier((core, crossing))
    crossed = shift(crossing, masks)
    others.append(swapped(cut_rows(*chunks[1], core)))

    by_position = order_table.reshape(positions, slots_dev)
    near = jnp.stack([by_position[position ^ mask, :batch] for mask in range(masks)])
    far = jnp.stack([by_position[mirror ^ mask, :batch] for mask in range(masks)])
    both = jnp.concatenate([near, far], axis=1)
    table_orders = jnp.concatenate([both.reshape(-1), by_position[:, batch:].reshape(-1)])
    half_orders = both[0]
    full_orders = by_position[position, batch:]

    hidden = w_in.shape[0]
    w_in_own = w_in.reshape(hidden, fields, 2, half_levels).transpose(0, 2, 1, 3).reshape(hidden, 2 * half)
    w_out_own = w_out.reshape(fields, 2, half_levels, hidden).transpose(1, 0, 2, 3).reshape(2 * half, hidden)
    weights = lax.dynamic_slice_in_dim(lat_weight * math.sqrt(2.0 / lon_count), core * own_rows, own_rows)
    table = transposed_table(table_orders, lon_count)
    network = (w_in_own * 0.5, 0.5 * b_in[:, None], w_out_own, table)

    def send(x):
        shape = (positions, x.size // (positions * x.shape[-2] * x.shape[-1])) + x.shape[-2:]
        return lax.all_to_all(x.reshape(shape), everyone, split_axis=0, concat_axis=0, tiled=True)

    def cores_apart(arrays):
        count = arrays[0].shape[0] // 2
        return shift(jnp.concatenate([x[count:] for x in arrays], axis=0), 1)

    def transformed(chunk):
        start, rows = chunks[chunk]
        *by_link, rest = forward(
            links,
            2 * pair,
            core_word,
            weights[start : start + rows],
            flat,
            lambda c: c * own_blocks + start // ROWS,
            others[chunk],
            *network,
        )
        return by_link, rest

    by_links, rests = [], []
    for chunk in range(len(chunks)):
        by_link, rest = transformed(chunk)
        if chunk == 0:
            rest, crossed, core, others[1] = lax.optimization_barrier((rest, crossed, core, others[1]))
            others += [swapped(cut_rows(*c, core)) for c in chunks[2:]]
        if chunk == 2:
            rests[1], rest = lax.optimization_barrier((rests[1], rest))
        by_links.append([shift(x, 2 * link) for link, x in enumerate(by_link)])
        rests.append(rest)
    full_pieces = [send(rests[0])]
    crossed_too = lax.ppermute(crossed, "member", [(m, m ^ 1) for m in range(members)])
    rests[1], crossed_too, full_pieces[0], by_links[0] = lax.optimization_barrier(
        (rests[1], crossed_too, full_pieces[0], by_links[0])
    )
    full_pieces.append(send(rests[1]))
    rests[2], full_pieces[1], by_links[1:] = lax.optimization_barrier(
        (rests[2], full_pieces[1], by_links[1:])
    )
    full_pieces.append(send(rests[2]))
    half_pieces = []
    for by_link in by_links:
        apart = cores_apart(by_link)
        half_pieces.append(
            [(apart, (mask // 2) * pair) if mask % 2 else (by_link[mask // 2], 0) for mask in range(masks)]
        )

    near_legendre = lax.dynamic_slice(legendre, (0, 0, side * half_lats), (batch, degree_count, half_lats))
    far_legendre = [jnp.where(turn == 0, x, y) for x, y in ((crossed, crossed_too), (crossed_too, crossed))]
    half_legendre = jnp.concatenate([near_legendre, *far_legendre], axis=0)
    to_modal, to_levels = mode_matrices(modes, fields, half_levels)
    depth_lanes = jnp.tile(jnp.pad(depths, (0, LANES - levels)), 2)[None, :]
    matrices = (*to_modal, *to_levels, depth_lanes)
    half_step = functools.partial(spectral_half, place=place, orders=half_orders, pieces=half_pieces)
    partial = half_step(batch, batch, legendre=half_legendre, got=None, matrices=None)
    sums = shift(partial, masks)
    values = half_step(0, batch, legendre=half_legendre, got=sums, matrices=matrices)
    full_pieces[-1], values = lax.optimization_barrier((full_pieces[-1], values))
    far_values = shift(values, masks)
    last_rows = ROWS
    main, last = spectral_full(batch, last_rows, full_orders, full_pieces, legendre, matrices)
    main, far_values = lax.optimization_barrier((main, far_values))
    main = join(send(main))
    bands = synthesis_half(
        0, masks, place, half_orders, half_legendre, jnp.concatenate([values, far_values], axis=0)
    )
    bands = [shift(join(x), 2 * link) for link, x in enumerate(bands)]
    apart = cores_apart(bands)
    last, apart = lax.optimization_barrier((last, apart))
    last = join(send(last))
    near_bands = [(apart, mask // 2) if mask % 2 else (bands[mask // 2], 0) for mask in range(masks)]
    flat_table = table.reshape(-1, lon_count)
    main_rows = lat_rows - last_rows
    bands_at = lambda row: [(array, pair, block, row) for array, block in near_bands]
    full_slots = positions * (slots_dev - batch)
    bands = bands_at(0) + [(main, full_slots, 0, 0)]
    result = inverse(bands, main_rows, flat_table, lat_rows, 0, None)
    bands = bands_at(main_rows) + [(last, full_slots, 0, 0)]
    result = inverse(bands, last_rows, flat_table, lat_rows, main_rows, result)
    return result.reshape(grid.shape)


def body(grid, w_in, b_in, w_out, lat_weight, legendre, order_table, modes, depths):
    fields, half_levels, lat_rows, lon_count = grid.shape
    slots_dev = legendre.shape[0]
    count = 2 * fields * half_levels
    tiled = (
        lax.axis_size("lev") == 2
        and lat_rows % (2 * ROWS) == 0
        and lat_rows == 6 * ROWS
        and count == LANES + LANES // 2
        and half_levels * 2 <= LANES
        and half_levels % ROWS == 0
        and lon_count % 512 == 0
        and slots_dev % 16 == 0
        and lax.axis_size("lat") == 8
        and lax.axis_size("member") % 2 == 0
    )
    chosen = tiled_body if tiled else plain_body
    return chosen(grid, w_in, b_in, w_out, lat_weight, legendre, order_table, modes, depths)


def solution(mesh):
    in_specs = (
        P("member", "lev", "lat", None),
        P(),
        P(),
        P(),
        P("lat"),
        P(("lat", "lev"), None, None),
        P(),
        P(),
        P(),
    )
    out_specs = P("member", "lev", "lat", None)
    return jax.shard_map(body, mesh=mesh, in_specs=in_specs, out_specs=out_specs, check_vma=False)
```

time: 948 us -> 915 us (0.965)
  blocking collectives: 142 us -> 0 us
  waiting for transfers between devices: 419 us -> 498 us
  Pallas kernels: 302 us -> 268 us
  starting transfers between devices: 28.6 us -> 58.9 us
  local copies, waits for them, and re-layouts: 40.9 us -> 64.1 us
  other arithmetic: 5.65 us -> 19.4 us
    ppermute x2 -> x23, waiting for transfers between devices: 0.01 us -> 450 us  [the longest x19 450 us: tiled_body(): lax.ppermute(x, everyone, pairs(mask))]
    all_to_all x5, waiting for transfers between devices: 419 us -> 47.8 us  [send(): lax.all_to_all(x.reshape(shape), everyone, split_axis=0, concat_axis=0, t...]
    all_to_all x1 -> x0, blocking collectives: 142 us -> none  [send(): lax.all_to_all(x.reshape(shape), everyone, split_axis=0, concat_axis=0, t...]
    pallas_call x4 -> x7, Pallas kernels: 252 us -> 217 us  [the longest x3 116 us: forward(): pl.pallas_call(forward_kernel, grid_spec=pltpu.PrefetchScalarGridSpec(num...]
    ppermute x2 -> x23, starting transfers between devices: 0.71 us -> 29.3 us  [the longest x19 27 us: tiled_body(): lax.ppermute(x, everyone, pairs(mask))]
    dynamic_slice x3 -> x6, local copies, waits for them, and re-layouts: 13.6 us -> 20.9 us  [the longest x3 14.8 us: cut_rows(): lax.dynamic_slice_in_dim(flat, (1 - core) * own_rows + start, rows, 1)]
    unnamed x47 -> x79, local copies, waits for them, and re-layouts: 19.5 us -> 18.1 us
  transfers between devices with their start and end apart: 7 -> 28, of which waited for: 5 -> 13; matrix products, arithmetic and copies ran while one was open for 4% -> 8% of each run, Pallas kernels for 31% -> 28%
where the time goes in v2:
time: 915 us; the launch traced here: 910 us
  waiting for transfers between devices  498 us (54%)
  Pallas kernels  268 us (29%)
  local copies, waits for them, and re-layouts  64.1 us (7%)
  starting transfers between devices  58.9 us (6%)
  other arithmetic  19.4 us (2%)
    ppermute x19, waiting for transfers between devices, tiled_body(): lax.ppermute(x, everyone, pairs(mask))  450 us
    pallas_call x3, Pallas kernels, forward(): pl.pallas_call(forward_kernel, grid_spec=pltpu.PrefetchScalarGridSpec(num...  116 us
    pallas_call x1, Pallas kernels, spectral_full(): pl.pallas_call(functools.partial(full_kernel, len(pieces)), grid_spec=plt...  70.9 us
    pallas_call x2, Pallas kernels, inverse(): pl.pallas_call(functools.partial(kernel, scale), grid=(rows // ROWS,), in...  50 us
    all_to_all x5, waiting for transfers between devices, send(): lax.all_to_all(x.reshape(shape), everyone, split_axis=0, concat_axis=0, t...  47.8 us
    all_to_all x5, starting transfers between devices, send(): lax.all_to_all(x.reshape(shape), everyone, split_axis=0, concat_axis=0, t...  29.6 us
    ppermute x19, starting transfers between devices, tiled_body(): lax.ppermute(x, everyone, pairs(mask))  27 us
    pallas_call x2, Pallas kernels, spectral_half(): pl.pallas_call(functools.partial(kernel, len(pieces), first_slot), grid_s...  19.3 us
  transfers between devices with their start and end apart: 28, of which 13 were waited for; matrix products, arithmetic and copies ran while one was open for 8% of the time, Pallas kernels for 28%

profile of v2, /device:TPU:11, one launch (start us, length us, event | category | flops | bytes accessed | tf_op | source)
XLA Modules:
  0.0 909.9 jit_solution(7298881001671783262)
XLA Ops:
  0.0 4.9 constant_dynamic-slice_fusion.3
  5.5 3.3 constant_dynamic-slice_fusion.2
  8.9 5.0 constant_dynamic-slice_fusion.1
  13.9 2.3 collective-permute-start.1
  19.7 1.1 fusion.5
  20.8 1.1 multiply_sine_fusion
  22.0 1.8 table.1.table_ref
  23.8 1.6 copy-done
  26.1 38.5 %forward.3 = (bf16[16,16,768]{2,1,0:T(8,128)(2,1)}, bf16[16,16,768]{2,1,0:T(8,128)(2,1)}, bf16[16,16,768]{2,1,0:T(8,128)(2,1)}, bf16[16,16,768]{2,1,0:T(8,128)(2,1)}, bf16[192,16,768]{2,1,0:T(8,128)(2,1)}) custom-call(s32[1]{0:T(128)} %bitcast.2.core_ref, f32[16]{0:T(128)} %get-tuple-element.142.weight_ref, bf16[96,96,1536]{2,1,0:T(8,128)(2,1)} %bitcast.48, ...), custom_call_target="tpu_custom_call" | custom-call | flops 1585446912 | bytes 983040 | tf_op jit(solution)/shard_map/forward/pallas_call | solution.py:250
  64.6 5.5 all-to-all-start
  70.2 4.9 constant_dynamic-slice_fusion
  75.5 1.2 collective-permute-start.4
  77.1 2.3 collective-permute-start.7
  79.4 39.0 %forward.4 = (bf16[16,16,768]{2,1,0:T(8,128)(2,1)}, bf16[16,16,768]{2,1,0:T(8,128)(2,1)}, bf16[16,16,768]{2,1,0:T(8,128)(2,1)}, bf16[16,16,768]{2,1,0:T(8,128)(2,1)}, bf16[192,16,768]{2,1,0:T(8,128)(2,1)}) custom-call(s32[1]{0:T(128)} %bitcast.2.core_ref, f32[16]{0:T(128)} %get-tuple-element.141.weight_ref, bf16[96,96,1536]{2,1,0:T(8,128)(2,1)} %bitcast.50, ...), custom_call_target="tpu_custom_call" | custom-call | flops 1585446912 | bytes 983040 | tf_op jit(solution)/shard_map/forward/pallas_call | solution.py:250
  118.4 38.5 %forward.5 = (bf16[16,16,768]{2,1,0:T(8,128)(2,1)}, bf16[16,16,768]{2,1,0:T(8,128)(2,1)}, bf16[16,16,768]{2,1,0:T(8,128)(2,1)}, bf16[16,16,768]{2,1,0:T(8,128)(2,1)}, bf16[192,16,768]{2,1,0:T(8,128)(2,1)}) custom-call(s32[1]{0:T(128)} %bitcast.2.core_ref, f32[16]{0:T(128)} %get-tuple-element.140.weight_ref, bf16[96,96,1536]{2,1,0:T(8,128)(2,1)} %bitcast.51, ...), custom_call_target="tpu_custom_call" | custom-call | flops 1585446912 | bytes 983040 | tf_op jit(solution)/shard_map/forward/pallas_call | solution.py:250
  156.9 7.3 collective-permute-done.7.refs_6_
  164.2 13.8 %all-to-all-done.refs_0_ = bf16[16,12,16,768]{3,2,1,0:T(8,128)(2,1)} async-done(((bf16[16,12,16,768]{3,2,1,0:T(8,128)(2,1)}), bf16[16,12,16,768]{3,2,1,0:T(8,128)(2,1)}, u32[]{:S(2)}, u32[]{:S(2)}) %all-to-all-start) | async-done | bytes 4718624 | tf_op jit(solution)/shard_map/all_to_all | solution.py:625
  178.0 4.6 all-to-all-start.1
  182.8 2.6 collective-permute-start.10
  185.6 31.6 %collective-permute-done.8.refs_10_ = bf16[16,16,768]{2,1,0:T(8,128)(2,1)S(1)} collective-permute-done((bf16[16,16,768]{2,1,0:T(8,128)(2,1)}, bf16[16,16,768]{2,1,0:T(8,128)(2,1)S(1)}, u32[]{:S(2)}, u32[]{:S(2)}) %collective-permute-start.8) | collective-permute-done | bytes 393248 | tf_op jit(solution)/shard_map/ppermute | solution.py:582
  217.2 9.2 %collective-permute-start.13 = (bf16[16,16,768]{2,1,0:T(8,128)(2,1)}, bf16[16,16,768]{2,1,0:T(8,128)(2,1)}, u32[]{:S(2)}, u32[]{:S(2)}) collective-permute-start(bf16[16,16,768]{2,1,0:T(8,128)(2,1)} %get-tuple-element.86), channel_id=1, source_target_pairs={{0,6},{1,7},{2,4},{3,5},{4,2},{5,3},{6,0},{7,1},{8,14},{9,15},{10,... | collective-permute-start | bytes 1179656 | tf_op jit(solution)/shard_map/ppermute | solution.py:582
  226.4 42.7 %collective-permute-done.9.refs_12_ = bf16[16,16,768]{2,1,0:T(8,128)(2,1)S(1)} collective-permute-done((bf16[16,16,768]{2,1,0:T(8,128)(2,1)}, bf16[16,16,768]{2,1,0:T(8,128)(2,1)S(1)}, u32[]{:S(2)}, u32[]{:S(2)}) %collective-permute-start.9) | collective-permute-done | bytes 393248 | tf_op jit(solution)/shard_map/ppermute | solution.py:582
  269.1 7.5 collective-permute-done.10.refs_14_
  276.6 12.6 %collective-permute-done.12.refs_20_ = bf16[16,16,768]{2,1,0:T(8,128)(2,1)S(1)} collective-permute-done((bf16[16,16,768]{2,1,0:T(8,128)(2,1)}, bf16[16,16,768]{2,1,0:T(8,128)(2,1)S(1)}, u32[]{:S(2)}, u32[]{:S(2)}) %collective-permute-start.12) | collective-permute-done | bytes 393248 | tf_op jit(solution)/shard_map/ppermute | solution.py:582
  289.2 5.3 collective-permute-done.13.refs_22_
  294.5 9.0 all-to-all-start.2
  303.5 12.1 %copy.71.refs_3_ = bf16[16,513,768]{2,1,0:T(8,128)(2,1)} copy(bf16[16,513,768]{2,0,1:T(8,128)(2,1)} %param.20) | data formatting | bytes 25214976 | tf_op args[5]
  317.1 1.0 slice.82
  319.3 1.0 pad_maximum_fusion.4
  320.7 2.7 constant_dynamic-slice_fusion.4
  323.4 1.8 broadcast_select_fusion.1
  325.3 2.2 pad_maximum_fusion.refs_24_.legendre_ref
  327.6 6.0 spectral_partial.1
  333.7 3.3 copy.85
  336.9 2.1 collective-permute-start.17
  340.2 2.4 gather_fusion.1
  342.6 1.8 copy.88
  345.0 2.4 gather_fusion
  347.4 1.7 copy.86
  349.2 2.0 broadcast_select_fusion.3
  351.2 2.3 copy.93
  353.5 1.1 broadcast_select_fusion.2
  354.6 2.6 subtract_convert_fusion
  358.2 114.2 %collective-permute-done.17 = bf16[4,513,384]{2,0,1:T(4,128)(2,1)} collective-permute-done((bf16[4,513,384]{2,0,1:T(4,128)(2,1)}, bf16[4,513,384]{2,0,1:T(4,128)(2,1)}, u32[]{:S(2)}, u32[]{:S(2)}) %collective-permute-start.17) | collective-permute-done | bytes 1575968 | tf_op jit(solution)/shard_map/ppermute | solution.py:582
  472.3 2.8 copy.89.refs_25_
  475.1 13.3 %spectral_update.1 = bf16[4,513,384]{2,1,0:T(8,128)(2,1)} custom-call(s32[1]{0:T(128)} %bitcast.place_ref, s32[8]{0:T(128)S(1)} %slice_bitcast_fusion.1.order_ref, bf16[16,16,768]{2,1,0:T(8,128)(2,1)S(1)} %copy-done.6, bf16[32,16,768]{2,1,0:T(8,128)(2,1)} %collective-permute-done.14.refs_1_.refs_3_.refs_5_.refs_7_, ...), custom_call_target="tpu_custom_call" | custom-call | flops 378224640 | bytes 245952 | tf_op jit(solution)/shard_map/spectral_update/pallas_call | solution.py:445
  488.5 2.1 copy.91
  490.6 3.2 collective-permute-start.18
  493.9 70.9 %spectral_full.1 = (bf16[16,12,80,384]{3,2,1,0:T(8,128)(2,1)}, bf16[16,12,16,384]{3,2,1,0:T(8,128)(2,1)}) custom-call(s32[12]{0:T(128)S(1)} %dynamic-slice_bitcast_fusion.order_ref, bf16[16,12,16,768]{3,2,1,0:T(8,128)(2,1)} %all-to-all-done.refs_0_, bf16[16,12,16,768]{3,2,1,0:T(8,128)(2,1)} %all-to-all-done.1.refs_1_, ...), custom_call_target="tpu_custom_call" | custom-call | flops 1815478272 | bytes 2360448 | tf_op jit(solution)/shard_map/spectral_full/pallas_call | solution.py:372
  564.8 6.0 all-to-all-start.4
  571.0 1.2 copy-done.19
  572.2 2.0 pad_maximum_fusion.1.values_ref
  574.2 10.3 %synthesis_half.1 = (bf16[2,8,96,384]{3,2,1,0:T(8,128)(2,1)S(1)}, bf16[2,8,96,384]{3,2,1,0:T(8,128)(2,1)S(1)}, bf16[2,8,96,384]{3,2,1,0:T(8,128)(2,1)S(1)}, bf16[2,8,96,384]{3,2,1,0:T(8,128)(2,1)}) custom-call(s32[1]{0:T(128)} %bitcast.place_ref, s32[8]{0:T(128)S(1)} %slice_bitcast_fusion.1.order_ref, ...), custom_call_target="tpu_custom_call" | custom-call | flops 151289856 | bytes 344448 | tf_op jit(solution)/shard_map/synthesis_half/pallas_call | solution.py:480
  584.9 2.3 collective-permute-start.21
  587.3 200.8 %collective-permute-done.20.refs_4_ = bf16[16,96,384]{2,1,0:T(8,128)(2,1)S(1)} collective-permute-done((bf16[16,96,384]{2,1,0:T(8,128)(2,1)S(1)}, bf16[16,96,384]{2,1,0:T(8,128)(2,1)S(1)}, u32[]{:S(2)}, u32[]{:S(2)}) %collective-permute-start.20) | collective-permute-done | bytes 1179680 | tf_op jit(solution)/shard_map/ppermute | solution.py:582
  790.1 24.3 %collective-permute-done.21.refs_6_ = bf16[16,96,384]{2,1,0:T(8,128)(2,1)S(1)} collective-permute-done((bf16[16,96,384]{2,1,0:T(8,128)(2,1)}, bf16[16,96,384]{2,1,0:T(8,128)(2,1)S(1)}, u32[]{:S(2)}, u32[]{:S(2)}) %collective-permute-start.21) | collective-permute-done | bytes 1179680 | tf_op jit(solution)/shard_map/ppermute | solution.py:582
  814.4 1.0 copy-done.22
  815.9 1.1 collective-permute-start.22
  817.0 4.2 collective-permute-done.22.refs_1_.refs_3_.refs_5_.refs_7_
  821.2 19.4 %all-to-all-done.4 = bf16[16,12,80,384]{3,2,1,0:T(8,128)(2,1)} async-done(((bf16[16,12,80,384]{3,2,1,0:T(8,128)(2,1)}), bf16[16,12,80,384]{3,2,1,0:T(8,128)(2,1)}, u32[]{:S(2)}, u32[]{:S(2)}) %all-to-all-start.4) | async-done | bytes 11796512 | tf_op jit(solution)/shard_map/all_to_all | solution.py:625
  840.6 4.5 all-to-all-start.3
  845.1 38.3 %inverse.2.refs_10_ = bf16[96,96,1536]{2,1,0:T(8,128)(2,1)} custom-call(bf16[16,96,384]{2,1,0:T(8,128)(2,1)} %bitcast.40, bf16[32,96,384]{2,1,0:T(8,128)(2,1)} %copy-done.18, bf16[16,96,384]{2,1,0:T(8,128)(2,1)} %copy-done.21, bf16[32,96,384]{2,1,0:T(8,128)(2,1)} %copy-done.18, bf16[16,96,384]{2,1,0:T(8,128)(2,1)} %copy-done.20, ...), custom_call_target="tpu_custom_call" | custom-call | flops 1509949440 | bytes 2457600 | tf_op jit(solution)/shard_map/inverse/pallas_call | solution.py:546
  883.4 14.6 %all-to-all-done.3 = bf16[16,12,16,384]{3,2,1,0:T(8,128)(2,1)} async-done(((bf16[16,12,16,384]{3,2,1,0:T(8,128)(2,1)}), bf16[16,12,16,384]{3,2,1,0:T(8,128)(2,1)}, u32[]{:S(2)}, u32[]{:S(2)}) %all-to-all-start.3) | async-done | bytes 2359328 | tf_op jit(solution)/shard_map/all_to_all | solution.py:625
  898.0 11.7 %inverse.3 = bf16[96,96,1536]{2,1,0:T(8,128)(2,1)} custom-call(bf16[16,96,384]{2,1,0:T(8,128)(2,1)} %bitcast.41, bf16[32,96,384]{2,1,0:T(8,128)(2,1)} %copy-done.18, bf16[16,96,384]{2,1,0:T(8,128)(2,1)} %copy-done.21, bf16[32,96,384]{2,1,0:T(8,128)(2,1)} %copy-done.18, bf16[16,96,384]{2,1,0:T(8,128)(2,1)} %copy-done.20, ...), custom_call_target="tpu_custom_call", output_to_operand_aliasing={{}: (10, {})} | custom-call | flops 301989888 | bytes 491520 | tf_op jit(solution)/shard_map/inverse/pallas_call | solution.py:546
  (158 shorter events, 15.0 us)
Async XLA Ops:
  4.9 21.2 %collective-permute-start = (bf16[96,16,1536]{2,1,0:T(8,128)(2,1)}, bf16[96,16,1536]{2,1,0:T(8,128)(2,1)}, u32[]{:S(2)}, u32[]{:S(2)}) collective-permute-start(bf16[96,16,1536]{2,1,0:T(8,128)(2,1)} %constant_dynamic-slice_fusion.3), channel_id=1, source_target_pairs={{0,1},{1,0},{2,3},{3,2},{4,5},{5,4},{6,7},{7,6},{8,9},{9,8},{10,11... | collective-permute-start | bytes 14155784 | tf_op jit(solution)/shard_map/ppermute | solution.py:590
  8.9 7.3 copy-start.31
  8.9 8.0 copy-start.26
  8.9 8.8 copy-start.27
  8.9 9.5 %copy-start.30 = (f32[384]{0:T(512)S(1)}, f32[384]{0:T(512)}, u32[]{:S(2)}) copy-start(f32[384]{0:T(512)} %param.17) | copy-start | bytes 4612
  8.9 10.7 %copy-start.36 = (f32[96]{0:T(128)S(1)}, f32[96]{0:T(128)}, u32[]{:S(2)}) copy-start(f32[96]{0:T(128)} %param.19) | copy-start | bytes 1156
  13.9 50.7 %collective-permute-start.2 = (bf16[96,16,1536]{2,1,0:T(8,128)(2,1)}, bf16[96,16,1536]{2,1,0:T(8,128)(2,1)}, u32[]{:S(2)}, u32[]{:S(2)}) collective-permute-start(bf16[96,16,1536]{2,1,0:T(8,128)(2,1)} %constant_dynamic-slice_fusion.1), channel_id=1, source_target_pairs={{0,1},{1,0},{2,3},{3,2},{4,5},{5,4},{6,7},{7,6},{8,9},{9,8},{10,11... | collective-permute-start | bytes 14155784 | tf_op jit(solution)/shard_map/ppermute | solution.py:590
  13.9 50.7 %collective-permute-start.1 = (bf16[2,513,384]{2,0,1:T(2,128)(2,1)S(1)}, bf16[2,513,384]{2,0,1:T(2,128)(2,1)S(1)}, u32[]{:S(2)}, u32[]{:S(2)}) collective-permute-start(bf16[2,513,384]{2,0,1:T(2,128)(2,1)S(1)} %constant_dynamic-slice_fusion.2), channel_id=1, source_target_pairs={{0,8},{1,9},{2,10},{3,11},{4,12},{5,13},{6,14},{7,15},{8,0},{9,1},... | collective-permute-start | bytes 2363912 | tf_op jit(solution)/shard_map/ppermute | solution.py:582
  64.6 10.9 %copy-start.25 = (bf16[2,513,384]{2,0,1:T(2,128)(2,1)}, bf16[2,513,384]{2,0,1:T(2,128)(2,1)S(1)}, u32[]{:S(2)}) copy-start(bf16[2,513,384]{2,0,1:T(2,128)(2,1)S(1)} %collective-permute-done.1) | copy-start | bytes 2363908
  64.6 113.4 %all-to-all-start = ((bf16[16,12,16,768]{3,2,1,0:T(8,128)(2,1)}), bf16[16,12,16,768]{3,2,1,0:T(8,128)(2,1)}, u32[]{:S(2)}, u32[]{:S(2)}) async-start(bf16[16,12,16,768]{3,2,1,0:T(8,128)(2,1)} %bitcast.54), calls=%async_computation | async-start | bytes 9437184 | tf_op jit(solution)/shard_map/all_to_all | solution.py:625
  70.2 6.6 copy-start.34
  70.2 6.8 copy-start.33
  70.2 6.9 copy-start.32
  75.2 43.2 %collective-permute-start.3 = (bf16[96,16,1536]{2,1,0:T(8,128)(2,1)}, bf16[96,16,1536]{2,1,0:T(8,128)(2,1)}, u32[]{:S(2)}, u32[]{:S(2)}) collective-permute-start(bf16[96,16,1536]{2,1,0:T(8,128)(2,1)} %constant_dynamic-slice_fusion), channel_id=1, source_target_pairs={{0,1},{1,0},{2,3},{3,2},{4,5},{5,4},{6,7},{7,6},{8,9},{9,8},{10,11... | collective-permute-start | bytes 14155784 | tf_op jit(solution)/shard_map/ppermute | solution.py:590
  75.5 88.7 %collective-permute-start.4 = (bf16[2,513,384]{2,0,1:T(2,128)(2,1)S(1)}, bf16[2,513,384]{2,0,1:T(2,128)(2,1)}, u32[]{:S(2)}, u32[]{:S(2)}) collective-permute-start(bf16[2,513,384]{2,0,1:T(2,128)(2,1)S(1)} %collective-permute-done.1), channel_id=1, source_target_pairs={{0,16},{16,0},{1,17},{17,1},{2,18},{18,2},{3,19},{19,3},{4,20},{20... | collective-permute-start | bytes 2363912 | tf_op jit(solution)/shard_map/ppermute | solution.py:656
  76.8 80.2 %collective-permute-start.5 = (bf16[16,16,768]{2,1,0:T(8,128)(2,1)S(1)}, bf16[16,16,768]{2,1,0:T(8,128)(2,1)S(1)}, u32[]{:S(2)}, u32[]{:S(2)}) collective-permute-start(bf16[16,16,768]{2,1,0:T(8,128)(2,1)S(1)} %copy-done.34), channel_id=1, source_target_pairs={{0,2},{1,3},{2,0},{3,1},{4,6},{5,7},{6,4},{7,5},{8,10},{9,11},{10,... | collective-permute-start | bytes 1179656 | tf_op jit(solution)/shard_map/ppermute | solution.py:582
  77.1 79.9 %collective-permute-start.6 = (bf16[16,16,768]{2,1,0:T(8,128)(2,1)S(1)}, bf16[16,16,768]{2,1,0:T(8,128)(2,1)S(1)}, u32[]{:S(2)}, u32[]{:S(2)}) collective-permute-start(bf16[16,16,768]{2,1,0:T(8,128)(2,1)S(1)} %copy-done.33), channel_id=1, source_target_pairs={{0,4},{1,5},{2,6},{3,7},{4,0},{5,1},{6,2},{7,3},{8,12},{9,13},{10,... | collective-permute-start | bytes 1179656 | tf_op jit(solution)/shard_map/ppermute | solution.py:582
  77.1 87.1 %collective-permute-start.7 = (bf16[16,16,768]{2,1,0:T(8,128)(2,1)S(1)}, bf16[16,16,768]{2,1,0:T(8,128)(2,1)S(1)}, u32[]{:S(2)}, u32[]{:S(2)}) collective-permute-start(bf16[16,16,768]{2,1,0:T(8,128)(2,1)S(1)} %copy-done.32), channel_id=1, source_target_pairs={{0,6},{1,7},{2,4},{3,5},{4,2},{5,3},{6,0},{7,1},{8,14},{9,15},{10,... | collective-permute-start | bytes 1179656 | tf_op jit(solution)/shard_map/ppermute | solution.py:582
  178.0 4.7 copy-start.35
  178.0 116.5 %all-to-all-start.1 = ((bf16[16,12,16,768]{3,2,1,0:T(8,128)(2,1)}), bf16[16,12,16,768]{3,2,1,0:T(8,128)(2,1)}, u32[]{:S(2)}, u32[]{:S(2)}) async-start(bf16[16,12,16,768]{3,2,1,0:T(8,128)(2,1)} %bitcast.53), calls=%async_computation.1 | async-start | bytes 9437184 | tf_op jit(solution)/shard_map/all_to_all | solution.py:625
  182.6 34.6 %collective-permute-start.8 = (bf16[16,16,768]{2,1,0:T(8,128)(2,1)}, bf16[16,16,768]{2,1,0:T(8,128)(2,1)S(1)}, u32[]{:S(2)}, u32[]{:S(2)}) collective-permute-start(bf16[16,16,768]{2,1,0:T(8,128)(2,1)} %get-tuple-element.80), channel_id=1, source_target_pairs={{0,2},{1,3},{2,0},{3,1},{4,6},{5,7},{6,4},{7,5},{8,10},{9,11},{10,... | collective-permute-start | bytes 1179656 | tf_op jit(solution)/shard_map/ppermute | solution.py:582
  182.7 86.4 %collective-permute-start.9 = (bf16[16,16,768]{2,1,0:T(8,128)(2,1)}, bf16[16,16,768]{2,1,0:T(8,128)(2,1)S(1)}, u32[]{:S(2)}, u32[]{:S(2)}) collective-permute-start(bf16[16,16,768]{2,1,0:T(8,128)(2,1)} %get-tuple-element.81), channel_id=1, source_target_pairs={{0,4},{1,5},{2,6},{3,7},{4,0},{5,1},{6,2},{7,3},{8,12},{9,13},{10,... | collective-permute-start | bytes 1179656 | tf_op jit(solution)/shard_map/ppermute | solution.py:582
  182.8 93.8 %collective-permute-start.10 = (bf16[16,16,768]{2,1,0:T(8,128)(2,1)S(1)}, bf16[16,16,768]{2,1,0:T(8,128)(2,1)S(1)}, u32[]{:S(2)}, u32[]{:S(2)}) collective-permute-start(bf16[16,16,768]{2,1,0:T(8,128)(2,1)S(1)} %copy-done.35), channel_id=1, source_target_pairs={{0,6},{1,7},{2,4},{3,5},{4,2},{5,3},{6,0},{7,1},{8,14},{9,15},{10,... | collective-permute-start | bytes 1179656 | tf_op jit(solution)/shard_map/ppermute | solution.py:582
  185.3 91.2 %collective-permute-start.11 = (bf16[16,16,768]{2,1,0:T(8,128)(2,1)}, bf16[16,16,768]{2,1,0:T(8,128)(2,1)S(1)}, u32[]{:S(2)}, u32[]{:S(2)}) collective-permute-start(bf16[16,16,768]{2,1,0:T(8,128)(2,1)} %get-tuple-element.84), channel_id=1, source_target_pairs={{0,2},{1,3},{2,0},{3,1},{4,6},{5,7},{6,4},{7,5},{8,10},{9,11},{10,... | collective-permute-start | bytes 1179656 | tf_op jit(solution)/shard_map/ppermute | solution.py:582
  185.4 103.8 %collective-permute-start.12 = (bf16[16,16,768]{2,1,0:T(8,128)(2,1)}, bf16[16,16,768]{2,1,0:T(8,128)(2,1)S(1)}, u32[]{:S(2)}, u32[]{:S(2)}) collective-permute-start(bf16[16,16,768]{2,1,0:T(8,128)(2,1)} %get-tuple-element.85), channel_id=1, source_target_pairs={{0,4},{1,5},{2,6},{3,7},{4,0},{5,1},{6,2},{7,3},{8,12},{9,13},{10,... | collective-permute-start | bytes 1179656 | tf_op jit(solution)/shard_map/ppermute | solution.py:582
  217.2 99.8 %copy-start.9 = (bf16[16,16,768]{2,1,0:T(8,128)(2,1)}, bf16[16,16,768]{2,1,0:T(8,128)(2,1)S(1)}, u32[]{:S(2)}) copy-start(bf16[16,16,768]{2,1,0:T(8,128)(2,1)S(1)} %collective-permute-done.8.refs_10_) | copy-start | bytes 1179652
  217.2 77.3 %collective-permute-start.13 = (bf16[16,16,768]{2,1,0:T(8,128)(2,1)}, bf16[16,16,768]{2,1,0:T(8,128)(2,1)}, u32[]{:S(2)}, u32[]{:S(2)}) collective-permute-start(bf16[16,16,768]{2,1,0:T(8,128)(2,1)} %get-tuple-element.86), channel_id=1, source_target_pairs={{0,6},{1,7},{2,4},{3,5},{4,2},{5,3},{6,0},{7,1},{8,14},{9,15},{10,... | collective-permute-start | bytes 1179656 | tf_op jit(solution)/shard_map/ppermute | solution.py:582
  269.1 48.0 %copy-start.11 = (bf16[16,16,768]{2,1,0:T(8,128)(2,1)}, bf16[16,16,768]{2,1,0:T(8,128)(2,1)S(1)}, u32[]{:S(2)}) copy-start(bf16[16,16,768]{2,1,0:T(8,128)(2,1)S(1)} %collective-permute-done.9.refs_12_) | copy-start | bytes 1179652
  276.6 40.5 %copy-start.13 = (bf16[16,16,768]{2,1,0:T(8,128)(2,1)}, bf16[16,16,768]{2,1,0:T(8,128)(2,1)S(1)}, u32[]{:S(2)}) copy-start(bf16[16,16,768]{2,1,0:T(8,128)(2,1)S(1)} %collective-permute-done.10.refs_14_) | copy-start | bytes 1179652
  276.6 17.9 %copy-start.15 = (bf16[16,16,768]{2,1,0:T(8,128)(2,1)}, bf16[16,16,768]{2,1,0:T(8,128)(2,1)S(1)}, u32[]{:S(2)}) copy-start(bf16[16,16,768]{2,1,0:T(8,128)(2,1)S(1)} %collective-permute-done.11.refs_18_) | copy-start | bytes 1179652
  289.2 5.3 copy-start.24
  294.5 194.0 %all-to-all-start.2 = ((bf16[16,12,16,768]{3,2,1,0:T(8,128)(2,1)}), bf16[16,12,16,768]{3,2,1,0:T(8,128)(2,1)}, u32[]{:S(2)}, u32[]{:S(2)}) async-start(bf16[16,12,16,768]{3,2,1,0:T(8,128)(2,1)} %bitcast.52), calls=%async_computation.2 | async-start | bytes 9437184 | tf_op jit(solution)/shard_map/all_to_all | solution.py:625
  303.5 12.1 %copy-start.6 = (bf16[16,16,768]{2,1,0:T(8,128)(2,1)S(1)}, bf16[16,16,768]{2,1,0:T(8,128)(2,1)}, u32[]{:S(2)}) copy-start(bf16[16,16,768]{2,1,0:T(8,128)(2,1)} %get-tuple-element.88.refs_0_) | copy-start | bytes 1179652
  315.5 2.6 slice-start.3
  315.6 2.6 slice-start.4
  316.6 10.9 %collective-permute-start.14 = (bf16[32,16,768]{2,1,0:T(8,128)(2,1)}, bf16[32,16,768]{2,1,0:T(8,128)(2,1)}, u32[]{:S(2)}, u32[]{:S(2)}) collective-permute-start(bf16[32,16,768]{2,1,0:T(8,128)(2,1)} %pad_maximum_fusion.3), channel_id=1, source_target_pairs={{0,1},{1,0},{2,3},{3,2},{4,5},{5,4},{6,7},{7,6},{8,9},{9,8},{10,11... | collective-permute-start | bytes 2359304 | tf_op jit(solution)/shard_map/ppermute | solution.py:582
  317.0 2.3 slice-start
  317.1 2.3 slice-start.1
  317.1 2.2 slice-start.2
  319.2 8.4 collective-permute-start.16
  320.4 7.2 collective-permute-start.15
  325.3 2.3 copy-start.10
  325.3 2.3 copy-start.12
  325.3 2.3 copy-start.14
  325.3 2.3 copy-start.16
  327.6 11.4 %copy-start.37 = (f32[96]{0:T(128)S(1)}, f32[96]{0:T(128)}, u32[]{:S(2)}) copy-start(f32[96]{0:T(128)} %param.23) | copy-start | bytes 1156
  333.6 5.9 copy-start.28
  333.6 6.5 copy-start.29
  336.9 135.4 %collective-permute-start.17 = (bf16[4,513,384]{2,0,1:T(4,128)(2,1)}, bf16[4,513,384]{2,0,1:T(4,128)(2,1)}, u32[]{:S(2)}, u32[]{:S(2)}) collective-permute-start(bf16[4,513,384]{2,0,1:T(4,128)(2,1)} %copy.85), channel_id=1, source_target_pairs={{0,8},{1,9},{2,10},{3,11},{4,12},{5,13},{6,14},{7,15},{8,0},{9,1},... | collective-permute-start | bytes 4727816 | tf_op jit(solution)/shard_map/ppermute | solution.py:582
  354.6 120.5 %copy-start.38 = (f32[128]{0:T(128)S(1)}, f32[128]{0:T(128)}, u32[]{:S(2)}) copy-start(f32[128]{0:T(128)} %pad.9) | copy-start | bytes 1540
  354.6 120.5 %copy-start.17 = (bf16[16,16,768]{2,1,0:T(8,128)(2,1)S(1)}, bf16[16,16,768]{2,1,0:T(8,128)(2,1)}, u32[]{:S(2)}) copy-start(bf16[16,16,768]{2,1,0:T(8,128)(2,1)} %copy-done.15) | copy-start | bytes 1179652
  488.4 5.4 copy-start.2
  488.4 5.4 copy-start.3
  488.5 5.4 copy-start.4
  488.5 5.4 copy-start.5
  490.6 74.2 %collective-permute-start.18 = (bf16[4,513,384]{2,0,1:T(4,128)(2,1)S(1)}, bf16[4,513,384]{2,0,1:T(4,128)(2,1)S(1)}, u32[]{:S(2)}, u32[]{:S(2)}) collective-permute-start(bf16[4,513,384]{2,0,1:T(4,128)(2,1)S(1)} %copy.91), channel_id=1, source_target_pairs={{0,8},{1,9},{2,10},{3,11},{4,12},{5,13},{6,14},{7,15},{8,0},{9,1},... | collective-permute-start | bytes 4727816 | tf_op jit(solution)/shard_map/ppermute | solution.py:582
  564.8 275.8 %all-to-all-start.4 = ((bf16[16,12,80,384]{3,2,1,0:T(8,128)(2,1)}), bf16[16,12,80,384]{3,2,1,0:T(8,128)(2,1)}, u32[]{:S(2)}, u32[]{:S(2)}) async-start(bf16[16,12,80,384]{3,2,1,0:T(8,128)(2,1)} %get-tuple-element.113), calls=%async_computation.4 | async-start | bytes 23592960 | tf_op jit(solution)/shard_map/all_to_all | solution.py:625
  584.6 231.4 %copy-start.1 = (bf16[2,8,96,384]{3,2,1,0:T(8,128)(2,1)}, bf16[2,8,96,384]{3,2,1,0:T(8,128)(2,1)S(1)}, u32[]{:S(2)}) copy-start(bf16[2,8,96,384]{3,2,1,0:T(8,128)(2,1)S(1)} %get-tuple-element.106) | copy-start | bytes 3538948
  584.6 203.5 %collective-permute-start.20 = (bf16[16,96,384]{2,1,0:T(8,128)(2,1)S(1)}, bf16[16,96,384]{2,1,0:T(8,128)(2,1)S(1)}, u32[]{:S(2)}, u32[]{:S(2)}) collective-permute-start(bf16[16,96,384]{2,1,0:T(8,128)(2,1)S(1)} %bitcast.45), channel_id=1, source_target_pairs={{0,4},{1,5},{2,6},{3,7},{4,0},{5,1},{6,2},{7,3},{8,12},{9,13},{10,... | collective-permute-start | bytes 3538952 | tf_op jit(solution)/shard_map/ppermute | solution.py:582
  584.9 203.3 %collective-permute-start.19 = (bf16[16,96,384]{2,1,0:T(8,128)(2,1)S(1)}, bf16[16,96,384]{2,1,0:T(8,128)(2,1)S(1)}, u32[]{:S(2)}, u32[]{:S(2)}) collective-permute-start(bf16[16,96,384]{2,1,0:T(8,128)(2,1)S(1)} %bitcast.44), channel_id=1, source_target_pairs={{0,2},{1,3},{2,0},{3,1},{4,6},{5,7},{6,4},{7,5},{8,10},{9,11},{10,... | collective-permute-start | bytes 3538952 | tf_op jit(solution)/shard_map/ppermute | solution.py:582
  584.9 229.5 %collective-permute-start.21 = (bf16[16,96,384]{2,1,0:T(8,128)(2,1)}, bf16[16,96,384]{2,1,0:T(8,128)(2,1)S(1)}, u32[]{:S(2)}, u32[]{:S(2)}) collective-permute-start(bf16[16,96,384]{2,1,0:T(8,128)(2,1)} %bitcast.62), channel_id=1, source_target_pairs={{0,6},{1,7},{2,4},{3,5},{4,2},{5,3},{6,0},{7,1},{8,14},{9,15},{10,... | collective-permute-start | bytes 3538952 | tf_op jit(solution)/shard_map/ppermute | solution.py:582
  815.9 5.2 collective-permute-start.22
  821.2 24.0 %copy-start.18 = (bf16[32,96,384]{2,1,0:T(8,128)(2,1)}, bf16[32,96,384]{2,1,0:T(8,128)(2,1)S(1)}, u32[]{:S(2)}) copy-start(bf16[32,96,384]{2,1,0:T(8,128)(2,1)S(1)} %collective-permute-done.22.refs_1_.refs_3_.refs_5_.refs_7_) | copy-start | bytes 7077892
  840.6 57.4 %all-to-all-start.3 = ((bf16[16,12,16,384]{3,2,1,0:T(8,128)(2,1)}), bf16[16,12,16,384]{3,2,1,0:T(8,128)(2,1)}, u32[]{:S(2)}, u32[]{:S(2)}) async-start(bf16[16,12,16,384]{3,2,1,0:T(8,128)(2,1)} %get-tuple-element.112), calls=%async_computation.3 | async-start | bytes 4718592 | tf_op jit(solution)/shard_map/all_to_all | solution.py:625
  (8 other events, 11.0 us)

commit v3 on v2

--- a/solution.py
+++ b/solution.py
@@ -110,9 +110,8 @@
     tail = count - LANES
     part = np.concatenate([np.repeat([0, 1], LANES), np.repeat([0, 1], tail)])
     item = np.concatenate([np.tile(np.arange(LANES), 2), np.tile(LANES + np.arange(tail), 2)])
-    half, rest = np.divmod(item, fields * half_levels)
-    field, level = np.divmod(rest, half_levels)
-    return part, field, half * half_levels + level
+    field, level = np.divmod(item, 2 * half_levels)
+    return part, field, level
 
 
 def synthesis_lanes(fields, half_levels):
@@ -153,12 +152,23 @@
     )
 
 
-def table_kernel(ca_ref, sa_ref, cb_ref, sb_ref, out_ref):
-    half = ca_ref.shape[0] // 2
-    for block in range(ca_ref.shape[1]):
+def table_kernel(orders_ref, out_ref):
+    half = out_ref.shape[1]
+    lon_count = out_ref.shape[2]
+    orders = orders_ref[...].astype(F32)
+
+    def turn(steps, width):
+        index = lax.broadcasted_iota(jnp.int32, (2 * half, width), 1).astype(F32)
+        product = orders * (index * steps)
+        phase = product - lon_count * jnp.floor(product * (1.0 / lon_count))
+        angle = phase * (2.0 * math.pi / lon_count)
+        return jnp.cos(angle), jnp.sin(angle)
+
+    cos_coarse, sin_coarse = turn(float(LANES), LANES)
+    cb, sb = turn(1.0, LANES)
+    for block in range(lon_count // LANES):
         lanes = slice(block * LANES, (block + 1) * LANES)
-        ca, sa = ca_ref[:, block : block + 1], sa_ref[:, block : block + 1]
-        cb, sb = cb_ref[...], sb_ref[...]
+        ca, sa = cos_coarse[:, block : block + 1], sin_coarse[:, block : block + 1]
         cos = (ca * cb - sa * sb).astype(BF16)
         sin = -(sa * cb + ca * sb).astype(BF16)
         out_ref[0, :, lanes] = cos[:half]
@@ -168,30 +178,28 @@
 
 
 def transposed_table(order_table, lon_count):
-    orders = jnp.concatenate([order_table, ORDERS - 1 - order_table]).astype(jnp.int32)
-    coarse = jnp.arange(lon_count // LANES, dtype=jnp.int32) * LANES
-    fine = jnp.arange(LANES, dtype=jnp.int32)
-    scale = 2.0 * math.pi / lon_count
-    angle_a = (orders[:, None] * coarse[None, :] % lon_count).astype(F32) * scale
-    angle_b = (orders[:, None] * fine[None, :] % lon_count).astype(F32) * scale
+    orders = jnp.concatenate([order_table, ORDERS - 1 - order_table])[:, None].astype(jnp.int32)
     return pl.pallas_call(
         table_kernel,
         out_shape=jax.ShapeDtypeStruct((4, order_table.shape[0], lon_count), BF16),
         compiler_params=pltpu.CompilerParams(vmem_limit_bytes=40 << 20),
         name="table",
-    )(jnp.cos(angle_a), jnp.sin(angle_a), jnp.cos(angle_b), jnp.sin(angle_b))
-
-
-def forward_kernel(core_ref, weight_ref, own_ref, other_ref, w_in_ref, b_in_ref, w_out_ref, table_ref, *refs):
+    )(orders)
+
+
+def forward_kernel(
+    half_levels, core_ref, weight_ref, own_ref, other_ref, w_in_ref, b_in_ref, w_out_ref, table_ref, *refs
+):
     outs, (columns, packed, even, odd) = refs[:-4], refs[-4:]
     core = core_ref[0]
     half = own_ref.shape[0]
     lon_count = own_ref.shape[2]
     slots = table_ref.shape[1]
-    own_at = pl.multiple_of(core * half, 32)
-    other_at = pl.multiple_of((1 - core) * half, 32)
-    columns[:, pl.ds(own_at, half), :] = jnp.swapaxes(own_ref[...], 0, 1)
-    columns[:, pl.ds(other_at, half), :] = jnp.swapaxes(other_ref[...], 0, 1)
+    for field in range(half // half_levels):
+        levels = slice(field * half_levels, (field + 1) * half_levels)
+        for place, source in ((core, own_ref), (1 - core, other_ref)):
+            at = pl.multiple_of((2 * field + place) * half_levels, ROWS)
+            columns[:, pl.ds(at, half_levels), :] = jnp.swapaxes(source[levels], 0, 1)
     lane = lax.broadcasted_iota(jnp.int32, (slots, LANES), 1)
 
     def network(r, state):
@@ -237,7 +245,7 @@
         at += out.shape[0]
 
 
-def forward(links, link_slots, core, weights, grid, first_block, other, w_in, b_in, w_out, table):
+def forward(half_levels, links, link_slots, core, weights, grid, first_block, other, w_in, b_in, w_out, table):
     half, rows, lon_count = other.shape
     slots = table.shape[1]
     hidden = w_in.shape[0]
@@ -248,7 +256,7 @@
     whole = lambda shape: pl.BlockSpec(shape, lambda i, *_: (0,) * len(shape), pipeline_mode=once)
     flops = 2 * rows * lon_count * (2 * 2 * half * hidden + 2 * half * 4 * slots)
     return pl.pallas_call(
-        forward_kernel,
+        functools.partial(forward_kernel, half_levels),
         grid_spec=pltpu.PrefetchScalarGridSpec(
             num_scalar_prefetch=2,
             grid=(rows // ROWS,),
@@ -288,11 +296,9 @@
 
 
 def product(values, high, low):
-    top, rest = split_wide(values)
-    return (
-        jnp.dot(top, high[...], preferred_element_type=F32)
-        + jnp.dot(rest, high[...], preferred_element_type=F32)
-        + jnp.dot(top, low[...], preferred_element_type=F32)
+    rounded = values.astype(BF16)
+    return jnp.dot(rounded, high[...], preferred_element_type=F32) + jnp.dot(
+        rounded, low[...], preferred_element_type=F32
     )
 
 
@@ -410,7 +416,7 @@
     gather_half(place_ref[0], pieces, blocks)
     order = order_ref[first_slot + pl.program_id(0)]
     analysed = jnp.dot(legendre_ref[0], blocks[...], preferred_element_type=F32)
-    out_ref[0] = select_orders(order, analysed).astype(BF16)
+    out_ref[0, : analysed.shape[0]] = select_orders(order, analysed).astype(BF16)
 
 
 def update_kernel(chunks, first_slot, place_ref, order_ref, *refs):
@@ -420,8 +426,9 @@
     gather_half(place_ref[0], pieces, blocks)
     order = order_ref[first_slot + pl.program_id(0)]
     analysed = jnp.dot(legendre_ref[0], blocks[...], preferred_element_type=F32)
-    spectral = select_orders(order, analysed) + got_ref[0].astype(F32)
-    out_ref[0] = implicit_lanes(order, spectral, *matrices)
+    degrees = analysed.shape[0]
+    spectral = select_orders(order, analysed) + got_ref[0, :degrees].astype(F32)
+    out_ref[0, :degrees] = implicit_lanes(order, spectral, *matrices)
 
 
 def spectral_half(first_slot, slots, place, orders, pieces, legendre, got, matrices):
@@ -432,7 +439,8 @@
     at_slot = lambda shape, base=0: pl.BlockSpec(
         (1,) + shape, lambda s, *_: (base + first_slot + s, 0, 0)
     )
-    plain = pl.BlockSpec((1, degrees, lanes // 2), lambda s, *_: (s, 0, 0))
+    tall = -(-degrees // ROWS) * ROWS
+    plain = pl.BlockSpec((1, tall, lanes // 2), lambda s, *_: (s, 0, 0))
     macs = slots * degrees * lat_count * lanes
     operands = flat + [legendre]
     in_specs = [at_slot(x.shape[1:], base) for x, base in zip(flat, bases)] + [at_slot((degrees, lat_count))]
@@ -451,7 +459,7 @@
             out_specs=plain,
             scratch_shapes=[pltpu.VMEM((lat_count, lanes), BF16)],
         ),
-        out_shape=jax.ShapeDtypeStruct((slots, degrees, lanes // 2), BF16),
+        out_shape=jax.ShapeDtypeStruct((slots, tall, lanes // 2), BF16),
         compiler_params=pltpu.CompilerParams(vmem_limit_bytes=50 << 20),
         cost_estimate=cost(
             flops=4 * macs, bytes_accessed=2 * slots * lat_count * (lanes + degrees), transcendentals=0
@@ -463,7 +471,8 @@
 def synthesis_kernel(first_slot, place_ref, order_ref, legendre_ref, values_ref, *refs):
     outs, bands = refs[:-1], refs[-1]
     order = order_ref[first_slot + pl.program_id(0)]
-    halves = band_halves(order, legendre_ref[0], values_ref[0])
+    legendre = legendre_ref[0]
+    halves = band_halves(order, legendre, values_ref[0, : legendre.shape[0]])
     lat_rows = bands.shape[1]
     for place in range(len(outs)):
         for half in range(2):
@@ -474,8 +483,8 @@
 
 
 def synthesis_half(first_slot, masks, place, orders, legendre, values):
-    slots, degrees, lanes = values.shape
-    lat_count = legendre.shape[2]
+    slots, tall, lanes = values.shape
+    _, degrees, lat_count = legendre.shape
     lat_rows = 2 * lat_count // masks
     return pl.pallas_call(
         functools.partial(synthesis_kernel, first_slot),
@@ -484,7 +493,7 @@
             grid=(slots,),
             in_specs=[
                 pl.BlockSpec((1, degrees, lat_count), lambda s, *_: (first_slot + s, 0, 0)),
-                pl.BlockSpec((1, degrees, lanes), lambda s, *_: (s, 0, 0)),
+                pl.BlockSpec((1, tall, lanes), lambda s, *_: (s, 0, 0)),
             ],
             out_specs=[pl.BlockSpec((2, 1, lat_rows, lanes), lambda s, *_: (0, s, 0, 0))] * (masks // 2),
             scratch_shapes=[pltpu.VMEM((masks, lat_rows, lanes), BF16)],
@@ -613,12 +622,9 @@
     half_orders = both[0]
     full_orders = by_position[position, batch:]
 
-    hidden = w_in.shape[0]
-    w_in_own = w_in.reshape(hidden, fields, 2, half_levels).transpose(0, 2, 1, 3).reshape(hidden, 2 * half)
-    w_out_own = w_out.reshape(fields, 2, half_levels, hidden).transpose(1, 0, 2, 3).reshape(2 * half, hidden)
     weights = lax.dynamic_slice_in_dim(lat_weight * math.sqrt(2.0 / lon_count), core * own_rows, own_rows)
     table = transposed_table(table_orders, lon_count)
-    network = (w_in_own * 0.5, 0.5 * b_in[:, None], w_out_own, table)
+    network = (w_in * 0.5, 0.5 * b_in[:, None], w_out, table)
 
     def send(x):
         shape = (positions, x.size // (positions * x.shape[-2] * x.shape[-1])) + x.shape[-2:]
@@ -631,6 +637,7 @@
     def transformed(chunk):
         start, rows = chunks[chunk]
         *by_link, rest = forward(
+            half_levels,
             links,
             2 * pair,
             core_word,
@@ -653,13 +660,14 @@
         by_links.append([shift(x, 2 * link) for link, x in enumerate(by_link)])
         rests.append(rest)
     full_pieces = [send(rests[0])]
+    rests[1], full_pieces[0], by_links[:2] = lax.optimization_barrier(
+        (rests[1], full_pieces[0], by_links[:2])
+    )
+    crossed, full_pieces[0] = lax.optimization_barrier((crossed, full_pieces[0]))
     crossed_too = lax.ppermute(crossed, "member", [(m, m ^ 1) for m in range(members)])
-    rests[1], crossed_too, full_pieces[0], by_links[0] = lax.optimization_barrier(
-        (rests[1], crossed_too, full_pieces[0], by_links[0])
-    )
     full_pieces.append(send(rests[1]))
-    rests[2], full_pieces[1], by_links[1:] = lax.optimization_barrier(
-        (rests[2], full_pieces[1], by_links[1:])
+    rests[2], crossed_too, full_pieces[1], by_links[2:] = lax.optimization_barrier(
+        (rests[2], crossed_too, full_pieces[1], by_links[2:])
     )
     full_pieces.append(send(rests[2]))
     half_pieces = []
@@ -676,17 +684,28 @@
     depth_lanes = jnp.tile(jnp.pad(depths, (0, LANES - levels)), 2)[None, :]
     matrices = (*to_modal, *to_levels, depth_lanes)
     half_step = functools.partial(spectral_half, place=place, orders=half_orders, pieces=half_pieces)
-    partial = half_step(batch, batch, legendre=half_legendre, got=None, matrices=None)
-    sums = shift(partial, masks)
-    values = half_step(0, batch, legendre=half_legendre, got=sums, matrices=matrices)
-    full_pieces[-1], values = lax.optimization_barrier((full_pieces[-1], values))
-    far_values = shift(values, masks)
+    near_values, far_values = [], []
+    partials = [
+        half_step(batch + part * share, share, legendre=half_legendre, got=None, matrices=None)
+        for part in range(2)
+    ]
+    partials[0], matrices = lax.optimization_barrier((partials[0], matrices))
+    first_sums = shift(partials[0], masks)
+    partials[1], first_sums = lax.optimization_barrier((partials[1], first_sums))
+    second_sums = shift(partials[1], masks)
+    for part, sums in enumerate((first_sums, second_sums)):
+        if part == 1:
+            sums, near_values[0] = lax.optimization_barrier((sums, near_values[0]))
+        values = half_step(part * share, share, legendre=half_legendre, got=sums, matrices=matrices)
+        near_values.append(values)
+        far_values.append(shift(values, masks))
+    full_pieces[-1], near_values = lax.optimization_barrier((full_pieces[-1], near_values))
     last_rows = ROWS
     main, last = spectral_full(batch, last_rows, full_orders, full_pieces, legendre, matrices)
     main, far_values = lax.optimization_barrier((main, far_values))
     main = join(send(main))
     bands = synthesis_half(
-        0, masks, place, half_orders, half_legendre, jnp.concatenate([values, far_values], axis=0)
+        0, masks, place, half_orders, half_legendre, jnp.concatenate([*near_values, *far_values], axis=0)
     )
     bands = [shift(join(x), 2 * link) for link, x in enumerate(bands)]
     apart = cores_apart(bands)

time: 915 us -> 916 us (level)
  waiting for transfers between devices: 498 us -> 525 us
  local copies, waits for them, and re-layouts: 64.1 us -> 50.8 us
  Pallas kernels: 268 us -> 257 us
    ppermute x19 -> x21, waiting for transfers between devices: 450 us -> 477 us  [tiled_body(): lax.ppermute(x, everyone, pairs(mask))]
    pallas_call x1, Pallas kernels: 70.9 us -> 56.8 us  [spectral_full(): pl.pallas_call(functools.partial(full_kernel, len(pieces)), grid_spec=plt...]
    ppermute x19 -> x21, starting transfers between devices: 27 us -> 23.7 us  [tiled_body(): lax.ppermute(x, everyone, pairs(mask))]
    unnamed x79 -> x86, local copies, waits for them, and re-layouts: 18.1 us -> 20.6 us
    pallas_call x2 -> x4, Pallas kernels: 19.3 us -> 21.5 us  [spectral_half(): pl.pallas_call(functools.partial(kernel, len(pieces), first_slot), grid_s...]
  transfers between devices with their start and end apart: 28 -> 30, of which waited for: 13 -> 14; matrix products, arithmetic and copies ran while one was open for 8% -> 6% of each run, Pallas kernels for 28% -> 27%
where the time goes in v3:
time: 916 us; the launch traced here: 908 us
  waiting for transfers between devices  525 us (57%)
  Pallas kernels  257 us (28%)
  starting transfers between devices  54.4 us (6%)
  local copies, waits for them, and re-layouts  50.8 us (6%)
  other arithmetic  19.3 us (2%)
    ppermute x21, waiting for transfers between devices, tiled_body(): lax.ppermute(x, everyone, pairs(mask))  477 us
    pallas_call x3, Pallas kernels, forward(): pl.pallas_call(functools.partial(forward_kernel, half_levels), grid_spec=...  115 us
    pallas_call x1, Pallas kernels, spectral_full(): pl.pallas_call(functools.partial(full_kernel, len(pieces)), grid_spec=plt...  56.8 us
    pallas_call x2, Pallas kernels, inverse(): pl.pallas_call(functools.partial(kernel, scale), grid=(rows // ROWS,), in...  50 us
    all_to_all x5, waiting for transfers between devices, send(): lax.all_to_all(x.reshape(shape), everyone, split_axis=0, concat_axis=0, t...  47.5 us
    all_to_all x5, starting transfers between devices, send(): lax.all_to_all(x.reshape(shape), everyone, split_axis=0, concat_axis=0, t...  28.5 us
    ppermute x21, starting transfers between devices, tiled_body(): lax.ppermute(x, everyone, pairs(mask))  23.7 us
    pallas_call x4, Pallas kernels, spectral_half(): pl.pallas_call(functools.partial(kernel, len(pieces), first_slot), grid_s...  21.5 us
  transfers between devices with their start and end apart: 30, of which 14 were waited for; matrix products, arithmetic and copies ran while one was open for 6% of the time, Pallas kernels for 27%

profile of v3, /device:TPU:11, one launch (start us, length us, event | category | flops | bytes accessed | tf_op | source)
XLA Modules:
  0.0 907.6 jit_solution(7462694451189336346)
XLA Ops:
  0.0 4.9 constant_dynamic-slice_fusion.3
  5.5 3.3 constant_dynamic-slice_fusion.2
  8.9 4.9 constant_dynamic-slice_fusion.1
  13.8 2.3 collective-permute-start.1
  18.1 3.7 table.1.table_ref
  21.8 1.6 copy-done
  24.9 38.3 %forward.3 = (bf16[16,16,768]{2,1,0:T(8,128)(2,1)}, bf16[16,16,768]{2,1,0:T(8,128)(2,1)}, bf16[16,16,768]{2,1,0:T(8,128)(2,1)}, bf16[16,16,768]{2,1,0:T(8,128)(2,1)}, bf16[192,16,768]{2,1,0:T(8,128)(2,1)}) custom-call(s32[1]{0:T(128)} %bitcast.2.core_ref, f32[16]{0:T(128)} %get-tuple-element.166.weight_ref, bf16[96,96,1536]{2,1,0:T(8,128)(2,1)} %bitcast.42, ...), custom_call_target="tpu_custom_call" | custom-call | flops 1585446912 | bytes 983040 | tf_op jit(solution)/shard_map/forward/pallas_call | solution.py:258
  64.1 5.2 all-to-all-start
  69.3 5.0 constant_dynamic-slice_fusion
  75.0 2.3 collective-permute-start.6
  77.3 38.6 %forward.4 = (bf16[16,16,768]{2,1,0:T(8,128)(2,1)}, bf16[16,16,768]{2,1,0:T(8,128)(2,1)}, bf16[16,16,768]{2,1,0:T(8,128)(2,1)}, bf16[16,16,768]{2,1,0:T(8,128)(2,1)}, bf16[192,16,768]{2,1,0:T(8,128)(2,1)}) custom-call(s32[1]{0:T(128)} %bitcast.2.core_ref, f32[16]{0:T(128)} %get-tuple-element.165.weight_ref, bf16[96,96,1536]{2,1,0:T(8,128)(2,1)} %bitcast.44, ...), custom_call_target="tpu_custom_call" | custom-call | flops 1585446912 | bytes 983040 | tf_op jit(solution)/shard_map/forward/pallas_call | solution.py:258
  116.3 2.3 collective-permute-start.9
  118.6 38.1 %forward.5 = (bf16[16,16,768]{2,1,0:T(8,128)(2,1)}, bf16[16,16,768]{2,1,0:T(8,128)(2,1)}, bf16[16,16,768]{2,1,0:T(8,128)(2,1)}, bf16[16,16,768]{2,1,0:T(8,128)(2,1)}, bf16[192,16,768]{2,1,0:T(8,128)(2,1)}) custom-call(s32[1]{0:T(128)} %bitcast.2.core_ref, f32[16]{0:T(128)} %get-tuple-element.164.weight_ref, bf16[96,96,1536]{2,1,0:T(8,128)(2,1)} %bitcast.45, ...), custom_call_target="tpu_custom_call" | custom-call | flops 1585446912 | bytes 983040 | tf_op jit(solution)/shard_map/forward/pallas_call | solution.py:258
  156.7 6.9 collective-permute-done.6.refs_6_
  163.6 12.4 %collective-permute-done.8.refs_12_ = bf16[16,16,768]{2,1,0:T(8,128)(2,1)S(1)} collective-permute-done((bf16[16,16,768]{2,1,0:T(8,128)(2,1)}, bf16[16,16,768]{2,1,0:T(8,128)(2,1)S(1)}, u32[]{:S(2)}, u32[]{:S(2)}) %collective-permute-start.8) | collective-permute-done | bytes 393248 | tf_op jit(solution)/shard_map/ppermute | solution.py:591
  175.9 5.4 collective-permute-done.9.refs_14_
  181.3 8.9 all-to-all-start.1
  190.2 1.2 collective-permute-start.10
  191.8 2.3 collective-permute-start.13
  194.1 31.1 %collective-permute-done.11.refs_18_ = bf16[16,16,768]{2,1,0:T(8,128)(2,1)S(1)} collective-permute-done((bf16[16,16,768]{2,1,0:T(8,128)(2,1)}, bf16[16,16,768]{2,1,0:T(8,128)(2,1)S(1)}, u32[]{:S(2)}, u32[]{:S(2)}) %collective-permute-start.11) | collective-permute-done | bytes 393248 | tf_op jit(solution)/shard_map/ppermute | solution.py:591
  225.2 51.8 %collective-permute-done.12.refs_20_ = bf16[16,16,768]{2,1,0:T(8,128)(2,1)} collective-permute-done((bf16[16,16,768]{2,1,0:T(8,128)(2,1)S(1)}, bf16[16,16,768]{2,1,0:T(8,128)(2,1)}, u32[]{:S(2)}, u32[]{:S(2)}) %collective-permute-start.12) | collective-permute-done | bytes 393248 | tf_op jit(solution)/shard_map/ppermute | solution.py:591
  277.0 7.6 collective-permute-done.13.refs_22_
  284.7 13.6 %all-to-all-done.1.refs_1_ = bf16[16,12,16,768]{3,2,1,0:T(8,128)(2,1)} async-done(((bf16[16,12,16,768]{3,2,1,0:T(8,128)(2,1)}), bf16[16,12,16,768]{3,2,1,0:T(8,128)(2,1)}, u32[]{:S(2)}, u32[]{:S(2)}) %all-to-all-start.1) | async-done | bytes 4718624 | tf_op jit(solution)/shard_map/all_to_all | solution.py:631
  298.2 4.6 all-to-all-start.2
  302.9 12.0 %copy.33.refs_3_ = bf16[16,513,768]{2,1,0:T(8,128)(2,1)} copy(bf16[16,513,768]{2,0,1:T(8,128)(2,1)} %param.20) | data formatting | bytes 25214976 | tf_op args[5]
  315.0 1.1 gather_fusion.1
  316.3 1.1 gather_fusion
  317.6 1.9 broadcast_select_fusion.3
  319.5 2.3 copy.47
  321.8 1.0 broadcast_select_fusion.2
  322.8 2.5 subtract_convert_fusion
  325.5 1.0 pad_maximum_fusion.4
  326.8 1.1 pad_maximum_fusion.3
  330.0 1.1 pad_maximum_fusion.5
  331.4 2.7 constant_dynamic-slice_fusion.4
  334.1 2.2 fusion
  336.3 1.7 broadcast_select_fusion.1
  338.0 2.2 pad_maximum_fusion.1.refs_24_.legendre_ref
  341.2 3.9 spectral_partial.3
  345.2 2.0 collective-permute-start.17
  347.1 3.9 spectral_partial.2
  351.0 88.1 %collective-permute-done.17.refs_25_ = bf16[2,528,384]{2,1,0:T(8,128)(2,1)S(1)} collective-permute-done((bf16[2,528,384]{2,1,0:T(8,128)(2,1)}, bf16[2,528,384]{2,1,0:T(8,128)(2,1)S(1)}, u32[]{:S(2)}, u32[]{:S(2)}) %collective-permute-start.17) | collective-permute-done | bytes 811040 | tf_op jit(solution)/shard_map/ppermute | solution.py:591
  439.2 3.0 collective-permute-start.18
  442.2 6.8 spectral_update.2
  449.0 1.0 collective-permute-start.19
  450.0 44.4 %collective-permute-done.18.refs_25_ = bf16[2,528,384]{2,1,0:T(8,128)(2,1)S(1)} collective-permute-done((bf16[2,528,384]{2,1,0:T(8,128)(2,1)}, bf16[2,528,384]{2,1,0:T(8,128)(2,1)S(1)}, u32[]{:S(2)}, u32[]{:S(2)}) %collective-permute-start.18) | collective-permute-done | bytes 811040 | tf_op jit(solution)/shard_map/ppermute | solution.py:591
  495.3 6.9 spectral_update.3
  502.2 3.1 collective-permute-start.20
  505.3 1.0 copy-done.16
  506.3 56.8 %spectral_full.1 = (bf16[16,12,80,384]{3,2,1,0:T(8,128)(2,1)}, bf16[16,12,16,384]{3,2,1,0:T(8,128)(2,1)}) custom-call(s32[12]{0:T(128)S(1)} %dynamic-slice_bitcast_fusion.order_ref, bf16[16,12,16,768]{3,2,1,0:T(8,128)(2,1)} %all-to-all-done.refs_0_, bf16[16,12,16,768]{3,2,1,0:T(8,128)(2,1)} %all-to-all-done.1.refs_1_, ...), custom_call_target="tpu_custom_call" | custom-call | flops 1815478272 | bytes 2360448 | tf_op jit(solution)/shard_map/spectral_full/pallas_call | solution.py:378
  563.2 5.2 all-to-all-start.4
  568.4 3.4 pad_maximum_fusion.values_ref
  571.8 10.4 %synthesis_half.1 = (bf16[2,8,96,384]{3,2,1,0:T(8,128)(2,1)S(1)}, bf16[2,8,96,384]{3,2,1,0:T(8,128)(2,1)S(1)}, bf16[2,8,96,384]{3,2,1,0:T(8,128)(2,1)S(1)}, bf16[2,8,96,384]{3,2,1,0:T(8,128)(2,1)}) custom-call(s32[1]{0:T(128)} %bitcast.place_ref, s32[8]{0:T(128)S(1)} %slice_bitcast_fusion.1.order_ref, ...), custom_call_target="tpu_custom_call" | custom-call | flops 151289856 | bytes 344448 | tf_op jit(solution)/shard_map/synthesis_half/pallas_call | solution.py:489
  582.5 2.3 collective-permute-start.23
  584.8 200.9 %collective-permute-done.22.refs_4_ = bf16[16,96,384]{2,1,0:T(8,128)(2,1)S(1)} collective-permute-done((bf16[16,96,384]{2,1,0:T(8,128)(2,1)S(1)}, bf16[16,96,384]{2,1,0:T(8,128)(2,1)S(1)}, u32[]{:S(2)}, u32[]{:S(2)}) %collective-permute-start.22) | collective-permute-done | bytes 1179680 | tf_op jit(solution)/shard_map/ppermute | solution.py:591
  787.8 24.2 %collective-permute-done.23.refs_6_ = bf16[16,96,384]{2,1,0:T(8,128)(2,1)S(1)} collective-permute-done((bf16[16,96,384]{2,1,0:T(8,128)(2,1)}, bf16[16,96,384]{2,1,0:T(8,128)(2,1)S(1)}, u32[]{:S(2)}, u32[]{:S(2)}) %collective-permute-start.23) | collective-permute-done | bytes 1179680 | tf_op jit(solution)/shard_map/ppermute | solution.py:591
  812.0 1.0 copy-done.21
  813.5 1.1 collective-permute-start.24
  814.6 4.2 collective-permute-done.24.refs_1_.refs_3_.refs_5_.refs_7_
  818.8 19.4 %all-to-all-done.4 = bf16[16,12,80,384]{3,2,1,0:T(8,128)(2,1)} async-done(((bf16[16,12,80,384]{3,2,1,0:T(8,128)(2,1)}), bf16[16,12,80,384]{3,2,1,0:T(8,128)(2,1)}, u32[]{:S(2)}, u32[]{:S(2)}) %all-to-all-start.4) | async-done | bytes 11796512 | tf_op jit(solution)/shard_map/all_to_all | solution.py:631
  838.1 4.6 all-to-all-start.3
  842.7 38.3 %inverse.2.refs_10_ = bf16[96,96,1536]{2,1,0:T(8,128)(2,1)} custom-call(bf16[16,96,384]{2,1,0:T(8,128)(2,1)} %bitcast.33, bf16[32,96,384]{2,1,0:T(8,128)(2,1)} %copy-done.18, bf16[16,96,384]{2,1,0:T(8,128)(2,1)} %copy-done.20, bf16[32,96,384]{2,1,0:T(8,128)(2,1)} %copy-done.18, bf16[16,96,384]{2,1,0:T(8,128)(2,1)} %copy-done.19, ...), custom_call_target="tpu_custom_call" | custom-call | flops 1509949440 | bytes 2457600 | tf_op jit(solution)/shard_map/inverse/pallas_call | solution.py:555
  881.0 14.6 %all-to-all-done.3 = bf16[16,12,16,384]{3,2,1,0:T(8,128)(2,1)} async-done(((bf16[16,12,16,384]{3,2,1,0:T(8,128)(2,1)}), bf16[16,12,16,384]{3,2,1,0:T(8,128)(2,1)}, u32[]{:S(2)}, u32[]{:S(2)}) %all-to-all-start.3) | async-done | bytes 2359328 | tf_op jit(solution)/shard_map/all_to_all | solution.py:631
  895.5 11.7 %inverse.3 = bf16[96,96,1536]{2,1,0:T(8,128)(2,1)} custom-call(bf16[16,96,384]{2,1,0:T(8,128)(2,1)} %bitcast.34, bf16[32,96,384]{2,1,0:T(8,128)(2,1)} %copy-done.18, bf16[16,96,384]{2,1,0:T(8,128)(2,1)} %copy-done.20, bf16[32,96,384]{2,1,0:T(8,128)(2,1)} %copy-done.18, bf16[16,96,384]{2,1,0:T(8,128)(2,1)} %copy-done.19, ...), custom_call_target="tpu_custom_call", output_to_operand_aliasing={{}: (10, {})} | custom-call | flops 301989888 | bytes 491520 | tf_op jit(solution)/shard_map/inverse/pallas_call | solution.py:555
  (159 shorter events, 14.3 us)
Async XLA Ops:
  4.9 20.0 %collective-permute-start = (bf16[96,16,1536]{2,1,0:T(8,128)(2,1)}, bf16[96,16,1536]{2,1,0:T(8,128)(2,1)}, u32[]{:S(2)}, u32[]{:S(2)}) collective-permute-start(bf16[96,16,1536]{2,1,0:T(8,128)(2,1)} %constant_dynamic-slice_fusion.3), channel_id=1, source_target_pairs={{0,1},{1,0},{2,3},{3,2},{4,5},{5,4},{6,7},{7,6},{8,9},{9,8},{10,11... | collective-permute-start | bytes 14155784 | tf_op jit(solution)/shard_map/ppermute | solution.py:599
  8.9 7.3 copy-start.34
  8.9 7.9 copy-start.33
  8.9 8.7 copy-start.29
  13.8 9.6 %copy-start.40 = (f32[96]{0:T(128)S(1)}, f32[96]{0:T(128)}, u32[]{:S(2)}) copy-start(f32[96]{0:T(128)} %param.19) | copy-start | bytes 1156
  13.8 49.4 %collective-permute-start.2 = (bf16[96,16,1536]{2,1,0:T(8,128)(2,1)}, bf16[96,16,1536]{2,1,0:T(8,128)(2,1)}, u32[]{:S(2)}, u32[]{:S(2)}) collective-permute-start(bf16[96,16,1536]{2,1,0:T(8,128)(2,1)} %constant_dynamic-slice_fusion.1), channel_id=1, source_target_pairs={{0,1},{1,0},{2,3},{3,2},{4,5},{5,4},{6,7},{7,6},{8,9},{9,8},{10,11... | collective-permute-start | bytes 14155784 | tf_op jit(solution)/shard_map/ppermute | solution.py:599
  13.8 49.4 %collective-permute-start.1 = (bf16[2,513,384]{2,0,1:T(2,128)(2,1)S(1)}, bf16[2,513,384]{2,0,1:T(2,128)(2,1)S(1)}, u32[]{:S(2)}, u32[]{:S(2)}) collective-permute-start(bf16[2,513,384]{2,0,1:T(2,128)(2,1)S(1)} %constant_dynamic-slice_fusion.2), channel_id=1, source_target_pairs={{0,8},{1,9},{2,10},{3,11},{4,12},{5,13},{6,14},{7,15},{8,0},{9,1},... | collective-permute-start | bytes 2363912 | tf_op jit(solution)/shard_map/ppermute | solution.py:591
  64.1 117.2 %all-to-all-start = ((bf16[16,12,16,768]{3,2,1,0:T(8,128)(2,1)}), bf16[16,12,16,768]{3,2,1,0:T(8,128)(2,1)}, u32[]{:S(2)}, u32[]{:S(2)}) async-start(bf16[16,12,16,768]{3,2,1,0:T(8,128)(2,1)} %bitcast.47), calls=%async_computation | async-start | bytes 9437184 | tf_op jit(solution)/shard_map/all_to_all | solution.py:631
  69.3 5.3 copy-start.37
  69.3 5.6 copy-start.36
  69.3 5.7 copy-start.35
  74.3 42.0 %collective-permute-start.3 = (bf16[96,16,1536]{2,1,0:T(8,128)(2,1)}, bf16[96,16,1536]{2,1,0:T(8,128)(2,1)}, u32[]{:S(2)}, u32[]{:S(2)}) collective-permute-start(bf16[96,16,1536]{2,1,0:T(8,128)(2,1)} %constant_dynamic-slice_fusion), channel_id=1, source_target_pairs={{0,1},{1,0},{2,3},{3,2},{4,5},{5,4},{6,7},{7,6},{8,9},{9,8},{10,11... | collective-permute-start | bytes 14155784 | tf_op jit(solution)/shard_map/ppermute | solution.py:599
  74.7 41.5 %collective-permute-start.4 = (bf16[16,16,768]{2,1,0:T(8,128)(2,1)S(1)}, bf16[16,16,768]{2,1,0:T(8,128)(2,1)S(1)}, u32[]{:S(2)}, u32[]{:S(2)}) collective-permute-start(bf16[16,16,768]{2,1,0:T(8,128)(2,1)S(1)} %copy-done.37), channel_id=1, source_target_pairs={{0,2},{1,3},{2,0},{3,1},{4,6},{5,7},{6,4},{7,5},{8,10},{9,11},{10,... | collective-permute-start | bytes 1179656 | tf_op jit(solution)/shard_map/ppermute | solution.py:591
  74.9 81.7 %collective-permute-start.5 = (bf16[16,16,768]{2,1,0:T(8,128)(2,1)S(1)}, bf16[16,16,768]{2,1,0:T(8,128)(2,1)S(1)}, u32[]{:S(2)}, u32[]{:S(2)}) collective-permute-start(bf16[16,16,768]{2,1,0:T(8,128)(2,1)S(1)} %copy-done.36), channel_id=1, source_target_pairs={{0,4},{1,5},{2,6},{3,7},{4,0},{5,1},{6,2},{7,3},{8,12},{9,13},{10,... | collective-permute-start | bytes 1179656 | tf_op jit(solution)/shard_map/ppermute | solution.py:591
  75.0 88.6 %collective-permute-start.6 = (bf16[16,16,768]{2,1,0:T(8,128)(2,1)S(1)}, bf16[16,16,768]{2,1,0:T(8,128)(2,1)S(1)}, u32[]{:S(2)}, u32[]{:S(2)}) collective-permute-start(bf16[16,16,768]{2,1,0:T(8,128)(2,1)S(1)} %copy-done.35), channel_id=1, source_target_pairs={{0,6},{1,7},{2,4},{3,5},{4,2},{5,3},{6,0},{7,1},{8,14},{9,15},{10,... | collective-permute-start | bytes 1179656 | tf_op jit(solution)/shard_map/ppermute | solution.py:591
  115.9 47.7 %collective-permute-start.7 = (bf16[16,16,768]{2,1,0:T(8,128)(2,1)}, bf16[16,16,768]{2,1,0:T(8,128)(2,1)S(1)}, u32[]{:S(2)}, u32[]{:S(2)}) collective-permute-start(bf16[16,16,768]{2,1,0:T(8,128)(2,1)} %get-tuple-element.91), channel_id=1, source_target_pairs={{0,2},{1,3},{2,0},{3,1},{4,6},{5,7},{6,4},{7,5},{8,10},{9,11},{10,... | collective-permute-start | bytes 1179656 | tf_op jit(solution)/shard_map/ppermute | solution.py:591
  116.2 209.2 %copy-start.2 = (bf16[16,16,768]{2,1,0:T(8,128)(2,1)}, bf16[16,16,768]{2,1,0:T(8,128)(2,1)S(1)}, u32[]{:S(2)}) copy-start(bf16[16,16,768]{2,1,0:T(8,128)(2,1)S(1)} %collective-permute-done.4.refs_2_) | copy-start | bytes 1179652
  116.2 59.7 %collective-permute-start.8 = (bf16[16,16,768]{2,1,0:T(8,128)(2,1)}, bf16[16,16,768]{2,1,0:T(8,128)(2,1)S(1)}, u32[]{:S(2)}, u32[]{:S(2)}) collective-permute-start(bf16[16,16,768]{2,1,0:T(8,128)(2,1)} %get-tuple-element.92), channel_id=1, source_target_pairs={{0,4},{1,5},{2,6},{3,7},{4,0},{5,1},{6,2},{7,3},{8,12},{9,13},{10,... | collective-permute-start | bytes 1179656 | tf_op jit(solution)/shard_map/ppermute | solution.py:591
  116.3 65.1 %collective-permute-start.9 = (bf16[16,16,768]{2,1,0:T(8,128)(2,1)}, bf16[16,16,768]{2,1,0:T(8,128)(2,1)S(1)}, u32[]{:S(2)}, u32[]{:S(2)}) collective-permute-start(bf16[16,16,768]{2,1,0:T(8,128)(2,1)} %get-tuple-element.93), channel_id=1, source_target_pairs={{0,6},{1,7},{2,4},{3,5},{4,2},{5,3},{6,0},{7,1},{8,14},{9,15},{10,... | collective-permute-start | bytes 1179656 | tf_op jit(solution)/shard_map/ppermute | solution.py:591
  156.7 168.7 %copy-start.4 = (bf16[16,16,768]{2,1,0:T(8,128)(2,1)}, bf16[16,16,768]{2,1,0:T(8,128)(2,1)S(1)}, u32[]{:S(2)}) copy-start(bf16[16,16,768]{2,1,0:T(8,128)(2,1)S(1)} %collective-permute-done.5.refs_4_) | copy-start | bytes 1179652
  163.6 161.8 %copy-start.6 = (bf16[16,16,768]{2,1,0:T(8,128)(2,1)}, bf16[16,16,768]{2,1,0:T(8,128)(2,1)S(1)}, u32[]{:S(2)}) copy-start(bf16[16,16,768]{2,1,0:T(8,128)(2,1)S(1)} %collective-permute-done.6.refs_6_) | copy-start | bytes 1179652
  181.3 10.4 %copy-start.39 = (bf16[16,16,768]{2,1,0:T(8,128)(2,1)S(1)}, bf16[16,16,768]{2,1,0:T(8,128)(2,1)}, u32[]{:S(2)}) copy-start(bf16[16,16,768]{2,1,0:T(8,128)(2,1)} %get-tuple-element.100) | copy-start | bytes 1179652
  181.3 10.5 %copy-start.38 = (bf16[16,16,768]{2,1,0:T(8,128)(2,1)S(1)}, bf16[16,16,768]{2,1,0:T(8,128)(2,1)}, u32[]{:S(2)}) copy-start(bf16[16,16,768]{2,1,0:T(8,128)(2,1)} %get-tuple-element.101) | copy-start | bytes 1179652
  181.3 116.9 %all-to-all-start.1 = ((bf16[16,12,16,768]{3,2,1,0:T(8,128)(2,1)}), bf16[16,12,16,768]{3,2,1,0:T(8,128)(2,1)}, u32[]{:S(2)}, u32[]{:S(2)}) async-start(bf16[16,12,16,768]{3,2,1,0:T(8,128)(2,1)} %bitcast.48), calls=%async_computation.1 | async-start | bytes 9437184 | tf_op jit(solution)/shard_map/all_to_all | solution.py:631
  190.2 94.4 %collective-permute-start.10 = (bf16[2,513,384]{2,0,1:T(2,128)(2,1)}, bf16[2,513,384]{2,0,1:T(2,128)(2,1)}, u32[]{:S(2)}, u32[]{:S(2)}) collective-permute-start(bf16[2,513,384]{2,0,1:T(2,128)(2,1)} %copy-done.27), channel_id=1, source_target_pairs={{0,16},{16,0},{1,17},{17,1},{2,18},{18,2},{3,19},{19,3},{4,20},{20... | collective-permute-start | bytes 2363912 | tf_op jit(solution)/shard_map/ppermute | solution.py:667
  191.5 33.7 %collective-permute-start.11 = (bf16[16,16,768]{2,1,0:T(8,128)(2,1)}, bf16[16,16,768]{2,1,0:T(8,128)(2,1)S(1)}, u32[]{:S(2)}, u32[]{:S(2)}) collective-permute-start(bf16[16,16,768]{2,1,0:T(8,128)(2,1)} %get-tuple-element.99), channel_id=1, source_target_pairs={{0,2},{1,3},{2,0},{3,1},{4,6},{5,7},{6,4},{7,5},{8,10},{9,11},{10,... | collective-permute-start | bytes 1179656 | tf_op jit(solution)/shard_map/ppermute | solution.py:591
  191.8 85.3 %collective-permute-start.12 = (bf16[16,16,768]{2,1,0:T(8,128)(2,1)S(1)}, bf16[16,16,768]{2,1,0:T(8,128)(2,1)}, u32[]{:S(2)}, u32[]{:S(2)}) collective-permute-start(bf16[16,16,768]{2,1,0:T(8,128)(2,1)S(1)} %copy-done.39), channel_id=1, source_target_pairs={{0,4},{1,5},{2,6},{3,7},{4,0},{5,1},{6,2},{7,3},{8,12},{9,13},{10,... | collective-permute-start | bytes 1179656 | tf_op jit(solution)/shard_map/ppermute | solution.py:591
  191.8 92.8 %collective-permute-start.13 = (bf16[16,16,768]{2,1,0:T(8,128)(2,1)S(1)}, bf16[16,16,768]{2,1,0:T(8,128)(2,1)}, u32[]{:S(2)}, u32[]{:S(2)}) collective-permute-start(bf16[16,16,768]{2,1,0:T(8,128)(2,1)S(1)} %copy-done.38), channel_id=1, source_target_pairs={{0,6},{1,7},{2,4},{3,5},{4,2},{5,3},{6,0},{7,1},{8,14},{9,15},{10,... | collective-permute-start | bytes 1179656 | tf_op jit(solution)/shard_map/ppermute | solution.py:591
  225.2 73.0 %copy-start.10 = (bf16[16,16,768]{2,1,0:T(8,128)(2,1)}, bf16[16,16,768]{2,1,0:T(8,128)(2,1)S(1)}, u32[]{:S(2)}) copy-start(bf16[16,16,768]{2,1,0:T(8,128)(2,1)S(1)} %collective-permute-done.11.refs_18_) | copy-start | bytes 1179652
  298.2 207.1 %all-to-all-start.2 = ((bf16[16,12,16,768]{3,2,1,0:T(8,128)(2,1)}), bf16[16,12,16,768]{3,2,1,0:T(8,128)(2,1)}, u32[]{:S(2)}, u32[]{:S(2)}) async-start(bf16[16,12,16,768]{3,2,1,0:T(8,128)(2,1)} %bitcast.46), calls=%async_computation.2 | async-start | bytes 9437184 | tf_op jit(solution)/shard_map/all_to_all | solution.py:631
  302.9 12.1 %copy-start.30 = (f32[96,96]{1,0:T(8,128)S(1)}, f32[96,96]{1,0:T(8,128)}, u32[]{:S(2)}) copy-start(f32[96,96]{1,0:T(8,128)} %param.22) | copy-start | bytes 110596
  302.9 12.1 %copy-start.32 = (s32[384]{0:T(512)S(1)}, s32[384]{0:T(512)}, u32[]{:S(2)}) copy-start(s32[384]{0:T(512)} %constant.131) | copy-start | bytes 4612
  302.9 13.3 %copy-start.31 = (s32[384]{0:T(512)S(1)}, s32[384]{0:T(512)}, u32[]{:S(2)}) copy-start(s32[384]{0:T(512)} %constant.130) | copy-start | bytes 4612
  315.0 6.8 copy-start.28
  317.4 7.9 copy-start.1
  319.5 5.9 copy-start.8
  325.4 4.6 slice-start.3
  326.5 13.8 %collective-permute-start.15 = (bf16[32,16,768]{2,1,0:T(8,128)(2,1)}, bf16[32,16,768]{2,1,0:T(8,128)(2,1)}, u32[]{:S(2)}, u32[]{:S(2)}) collective-permute-start(bf16[32,16,768]{2,1,0:T(8,128)(2,1)} %pad_maximum_fusion.4), channel_id=1, source_target_pairs={{0,1},{1,0},{2,3},{3,2},{4,5},{5,4},{6,7},{7,6},{8,9},{9,8},{10,11... | collective-permute-start | bytes 2359304 | tf_op jit(solution)/shard_map/ppermute | solution.py:591
  327.9 6.2 copy-start.41
  327.9 12.4 %collective-permute-start.14 = (bf16[32,16,768]{2,1,0:T(8,128)(2,1)}, bf16[32,16,768]{2,1,0:T(8,128)(2,1)}, u32[]{:S(2)}, u32[]{:S(2)}) collective-permute-start(bf16[32,16,768]{2,1,0:T(8,128)(2,1)} %pad_maximum_fusion.3), channel_id=1, source_target_pairs={{0,1},{1,0},{2,3},{3,2},{4,5},{5,4},{6,7},{7,6},{8,9},{9,8},{10,11... | collective-permute-start | bytes 2359304 | tf_op jit(solution)/shard_map/ppermute | solution.py:591
  331.1 9.2 %collective-permute-start.16 = (bf16[32,16,768]{2,1,0:T(8,128)(2,1)}, bf16[32,16,768]{2,1,0:T(8,128)(2,1)S(1)}, u32[]{:S(2)}, u32[]{:S(2)}) collective-permute-start(bf16[32,16,768]{2,1,0:T(8,128)(2,1)} %pad_maximum_fusion.5), channel_id=1, source_target_pairs={{0,1},{1,0},{2,3},{3,2},{4,5},{5,4},{6,7},{7,6},{8,9},{9,8},{10,11... | collective-permute-start | bytes 2359304 | tf_op jit(solution)/shard_map/ppermute | solution.py:591
  334.1 3.9 copy-start.22
  338.0 3.3 copy-start.3
  338.0 3.2 copy-start.5
  338.0 3.2 copy-start.7
  338.0 3.2 copy-start.11
  345.2 94.0 %collective-permute-start.17 = (bf16[2,528,384]{2,1,0:T(8,128)(2,1)}, bf16[2,528,384]{2,1,0:T(8,128)(2,1)S(1)}, u32[]{:S(2)}, u32[]{:S(2)}) collective-permute-start(bf16[2,528,384]{2,1,0:T(8,128)(2,1)} %spectral_partial.3), channel_id=1, source_target_pairs={{0,8},{1,9},{2,10},{3,11},{4,12},{5,13},{6,14},{7,15},{8,0},{9,1},... | collective-permute-start | bytes 2433032 | tf_op jit(solution)/shard_map/ppermute | solution.py:591
  439.2 3.0 copy-start.26
  439.2 55.2 %collective-permute-start.18 = (bf16[2,528,384]{2,1,0:T(8,128)(2,1)}, bf16[2,528,384]{2,1,0:T(8,128)(2,1)S(1)}, u32[]{:S(2)}, u32[]{:S(2)}) collective-permute-start(bf16[2,528,384]{2,1,0:T(8,128)(2,1)} %spectral_partial.2), channel_id=1, source_target_pairs={{0,8},{1,9},{2,10},{3,11},{4,12},{5,13},{6,14},{7,15},{8,0},{9,1},... | collective-permute-start | bytes 2433032 | tf_op jit(solution)/shard_map/ppermute | solution.py:591
  449.0 56.3 %copy-start.13 = (bf16[384,512]{1,0:T(8,128)(2,1)S(1)}, bf16[384,512]{1,0:T(8,128)(2,1)}, u32[]{:S(2)}) copy-start(bf16[384,512]{1,0:T(8,128)(2,1)} %get-tuple-element.120.refs_27_.refs_5_) | copy-start | bytes 1179652
  449.0 56.3 %copy-start.14 = (bf16[384,512]{1,0:T(8,128)(2,1)S(1)}, bf16[384,512]{1,0:T(8,128)(2,1)}, u32[]{:S(2)}) copy-start(bf16[384,512]{1,0:T(8,128)(2,1)} %get-tuple-element.119.refs_26_.refs_4_) | copy-start | bytes 1179652
  449.0 56.3 %copy-start.15 = (bf16[512,384]{1,0:T(8,128)(2,1)S(1)}, bf16[512,384]{1,0:T(8,128)(2,1)}, u32[]{:S(2)}) copy-start(bf16[512,384]{1,0:T(8,128)(2,1)} %get-tuple-element.122.refs_29_.refs_7_) | copy-start | bytes 1179652
  449.0 114.1 %collective-permute-start.19 = (bf16[2,528,384]{2,1,0:T(8,128)(2,1)}, bf16[2,528,384]{2,1,0:T(8,128)(2,1)}, u32[]{:S(2)}, u32[]{:S(2)}) collective-permute-start(bf16[2,528,384]{2,1,0:T(8,128)(2,1)} %spectral_update.2), channel_id=1, source_target_pairs={{0,8},{1,9},{2,10},{3,11},{4,12},{5,13},{6,14},{7,15},{8,0},{9,1},... | collective-permute-start | bytes 2433032 | tf_op jit(solution)/shard_map/ppermute | solution.py:591
  502.2 61.0 %collective-permute-start.20 = (bf16[2,528,384]{2,1,0:T(8,128)(2,1)}, bf16[2,528,384]{2,1,0:T(8,128)(2,1)S(1)}, u32[]{:S(2)}, u32[]{:S(2)}) collective-permute-start(bf16[2,528,384]{2,1,0:T(8,128)(2,1)} %spectral_update.3), channel_id=1, source_target_pairs={{0,8},{1,9},{2,10},{3,11},{4,12},{5,13},{6,14},{7,15},{8,0},{9,1},... | collective-permute-start | bytes 2433032 | tf_op jit(solution)/shard_map/ppermute | solution.py:591
  563.1 5.2 copy-start.23
  563.2 5.2 copy-start.24
  563.2 275.0 %all-to-all-start.4 = ((bf16[16,12,80,384]{3,2,1,0:T(8,128)(2,1)}), bf16[16,12,80,384]{3,2,1,0:T(8,128)(2,1)}, u32[]{:S(2)}, u32[]{:S(2)}) async-start(bf16[16,12,80,384]{3,2,1,0:T(8,128)(2,1)} %get-tuple-element.141), calls=%async_computation.4 | async-start | bytes 23592960 | tf_op jit(solution)/shard_map/all_to_all | solution.py:631
  582.1 231.4 %copy-start.12 = (bf16[2,8,96,384]{3,2,1,0:T(8,128)(2,1)}, bf16[2,8,96,384]{3,2,1,0:T(8,128)(2,1)S(1)}, u32[]{:S(2)}) copy-start(bf16[2,8,96,384]{3,2,1,0:T(8,128)(2,1)S(1)} %get-tuple-element.134) | copy-start | bytes 3538948
  582.1 203.6 %collective-permute-start.22 = (bf16[16,96,384]{2,1,0:T(8,128)(2,1)S(1)}, bf16[16,96,384]{2,1,0:T(8,128)(2,1)S(1)}, u32[]{:S(2)}, u32[]{:S(2)}) collective-permute-start(bf16[16,96,384]{2,1,0:T(8,128)(2,1)S(1)} %bitcast.39), channel_id=1, source_target_pairs={{0,4},{1,5},{2,6},{3,7},{4,0},{5,1},{6,2},{7,3},{8,12},{9,13},{10,... | collective-permute-start | bytes 3538952 | tf_op jit(solution)/shard_map/ppermute | solution.py:591
  582.4 203.4 %collective-permute-start.21 = (bf16[16,96,384]{2,1,0:T(8,128)(2,1)S(1)}, bf16[16,96,384]{2,1,0:T(8,128)(2,1)S(1)}, u32[]{:S(2)}, u32[]{:S(2)}) collective-permute-start(bf16[16,96,384]{2,1,0:T(8,128)(2,1)S(1)} %bitcast.38), channel_id=1, source_target_pairs={{0,2},{1,3},{2,0},{3,1},{4,6},{5,7},{6,4},{7,5},{8,10},{9,11},{10,... | collective-permute-start | bytes 3538952 | tf_op jit(solution)/shard_map/ppermute | solution.py:591
  582.5 229.5 %collective-permute-start.23 = (bf16[16,96,384]{2,1,0:T(8,128)(2,1)}, bf16[16,96,384]{2,1,0:T(8,128)(2,1)S(1)}, u32[]{:S(2)}, u32[]{:S(2)}) collective-permute-start(bf16[16,96,384]{2,1,0:T(8,128)(2,1)} %bitcast.51), channel_id=1, source_target_pairs={{0,6},{1,7},{2,4},{3,5},{4,2},{5,3},{6,0},{7,1},{8,14},{9,15},{10,... | collective-permute-start | bytes 3538952 | tf_op jit(solution)/shard_map/ppermute | solution.py:591
  813.5 5.2 collective-permute-start.24
  818.8 23.9 %copy-start.18 = (bf16[32,96,384]{2,1,0:T(8,128)(2,1)}, bf16[32,96,384]{2,1,0:T(8,128)(2,1)S(1)}, u32[]{:S(2)}) copy-start(bf16[32,96,384]{2,1,0:T(8,128)(2,1)S(1)} %collective-permute-done.24.refs_1_.refs_3_.refs_5_.refs_7_) | copy-start | bytes 7077892
  838.1 57.4 %all-to-all-start.3 = ((bf16[16,12,16,384]{3,2,1,0:T(8,128)(2,1)}), bf16[16,12,16,384]{3,2,1,0:T(8,128)(2,1)}, u32[]{:S(2)}, u32[]{:S(2)}) async-start(bf16[16,12,16,384]{3,2,1,0:T(8,128)(2,1)} %get-tuple-element.140), calls=%async_computation.3 | async-start | bytes 4718592 | tf_op jit(solution)/shard_map/all_to_all | solution.py:631
  (12 other events, 15.3 us)
